TPU v7x, 256 devices: a whole 4x4x8 slice. The times are simulated.
256 devices in a mesh: frame: 4 (over y_hi, core), slab: 64 (over x, z, y_lo).
Axes of the slice: x: 4, y: 4 (y_hi: 2, y_lo: 2; y = y_hi * 2 + y_lo), z: 8, core: 2. Of those that a mesh axis runs over, the one named last changes fastest.
Arguments:
- latents: bfloat16 [4, 128, 128, 256], P('frame', 'slab'), may hold values from -6 to 6
- conv_weight: bfloat16 [2304, 256], replicated, may hold values from -0.125 to 0.125
- conv_bias: float32 [256], replicated, may hold values from -3 to 3
- out_weight: bfloat16 [3, 2304], replicated, may hold values from -0.125 to 0.125
- row_table: int32 [4, 224], P('frame'), may hold values from 0 to 255, as said below
- patch_weight: bfloat16 [588, 1280], replicated, may hold values from -0.25 to 0.25
- pos_embed: bfloat16 [256, 1280], replicated, may hold values from -3 to 3
- proj_weight: bfloat16 [1280, 1024], replicated, may hold values from -0.15625 to 0.15625
- text_embed: float32 [1024], replicated, may hold values from -6 to 6
Outputs:
- reward: float32 [4], P('frame')
- grad_conv: float32 [2304, 256], P('slab')
- grad_out: float32 [3, 2304], replicated
Inputs may be any that keep to these rules, and one draw needn't show every extreme that they name: row_table[f, 0] = 0, each row of row_table never falls, row_table[f, 223] = min(255, 255), and every other row_table[f, i] is (i * 256) // 224 or one more, capped by the cummulative order.
All inputs are finite; a program needn't handle non-finite values.
Results may differ from a plain program's by a relative error of at most 0.0038.
Values may be sent and summed in bfloat16 or wider, within the bound.
A program may use at most 128 MiB of HBM per device.

v0:
```python
import jax
import jax.numpy as jnp
from jax import lax
from jax.sharding import PartitionSpec as P

IMG = 224
PATCH = 14


loss_scale = 256.0
norm_eps = 1e-05


def with_halo(block, sides, width):
    for axis, dim in sides:
        count = lax.axis_size(axis)
        forward = [(i, i + 1) for i in range(count - 1)]
        backward = [(target, source) for source, target in forward]
        low = lax.ppermute(
            lax.slice_in_dim(block, block.shape[dim] - width, None, axis=dim), axis, forward
        )
        high = lax.ppermute(lax.slice_in_dim(block, 0, width, axis=dim), axis, backward)
        block = jnp.concatenate([low, block, high], axis=dim)
    return block


def layer_normed(values):
    centred = values - jnp.mean(values, axis=-1, keepdims=True)
    return centred / jnp.sqrt(jnp.mean(centred * centred, axis=-1, keepdims=True) + norm_eps)


def clip_reward(crop_input, patch_weight, pos_embed, proj_weight, text_embed):
    grid_side = IMG // PATCH
    patches = crop_input.reshape(3, grid_side, PATCH, grid_side, PATCH).transpose(1, 3, 0, 2, 4)
    patches = patches.reshape(grid_side * grid_side, 3 * PATCH * PATCH)
    embedded = jnp.dot(patches, patch_weight.astype(jnp.float32), precision=lax.Precision.HIGHEST)
    embedded = embedded + pos_embed.astype(jnp.float32)
    pooled = jnp.mean(layer_normed(embedded), axis=0)
    projected = jnp.dot(
        layer_normed(pooled), proj_weight.astype(jnp.float32), precision=lax.Precision.HIGHEST
    )
    numer = jnp.sum(projected * text_embed)
    return numer / jnp.sqrt(
        (jnp.sum(projected * projected) + 1e-06) * (jnp.sum(text_embed * text_embed) + 1e-06)
    )


def row_weights(table, height):
    following = jnp.concatenate([table[1:], jnp.full((1,), height, jnp.int32)])
    upper = jnp.maximum(following, table + 1)
    rows = jnp.arange(height, dtype=jnp.int32)
    inside = (rows[None, :] >= table[:, None]) & (rows[None, :] < upper[:, None])
    counts = (upper - table).astype(jnp.float32)
    return jnp.where(inside, 1.0, 0.0).astype(jnp.float32) / counts[:, None]


def upsample(values):
    return jnp.repeat(jnp.repeat(values, 2, axis=0), 2, axis=1)


def column_pad(values):
    return jnp.pad(values, ((0, 0), (1, 1), (0, 0)))


def conv_hidden(padded, weight, row_count, col_count):
    channels = padded.shape[-1]
    summed = jnp.zeros((row_count * col_count, weight.shape[1]), jnp.float32)
    for tap_index in range(9):
        row_shift, col_shift = (tap_index // 3, tap_index % 3)
        window = padded[
            row_shift : row_shift + row_count, col_shift : col_shift + col_count
        ].reshape(row_count * col_count, channels)
        summed = summed + jnp.dot(
            window,
            weight[tap_index * channels : (tap_index + 1) * channels],
            preferred_element_type=jnp.float32,
        )
    return summed


def conv_image(padded, weight, row_count, col_count):
    channels = padded.shape[-1]
    summed = jnp.zeros((3, row_count * col_count), jnp.float32)
    for tap_index in range(9):
        row_shift, col_shift = (tap_index // 3, tap_index % 3)
        window = padded[
            row_shift : row_shift + row_count, col_shift : col_shift + col_count
        ].reshape(row_count * col_count, channels)
        summed = summed + lax.dot_general(
            weight[:, tap_index * channels : (tap_index + 1) * channels],
            window,
            (((1,), (1,)), ((), ())),
            preferred_element_type=jnp.float32,
        )
    return summed


def image_grad_to_hidden(grad_pad, weight, row_count, col_count):
    channels = weight.shape[1] // 9
    summed = jnp.zeros((row_count * col_count, channels), jnp.float32)
    for tap_index in range(9):
        row_shift, col_shift = (tap_index // 3, tap_index % 3)
        window = grad_pad[
            :, 2 - row_shift : 2 - row_shift + row_count, 2 - col_shift : 2 - col_shift + col_count
        ].reshape(3, row_count * col_count)
        summed = summed + lax.dot_general(
            window,
            weight[:, tap_index * channels : (tap_index + 1) * channels],
            (((0,), (0,)), ((), ())),
            preferred_element_type=jnp.float32,
        )
    return summed


def kernel_grad(padded, conv_grad, row_count, col_count):
    channels = padded.shape[-1]
    blocks = []
    for tap_index in range(9):
        row_shift, col_shift = (tap_index // 3, tap_index % 3)
        window = padded[
            row_shift : row_shift + row_count, col_shift : col_shift + col_count
        ].reshape(row_count * col_count, channels)
        blocks.append(
            lax.dot_general(
                window, conv_grad, (((0,), (0,)), ((), ())), preferred_element_type=jnp.float32
            )
        )
    return jnp.concatenate(blocks, axis=0)


def out_kernel_grad(grad_flat, hidden_pad, row_count, col_count):
    channels = hidden_pad.shape[-1]
    blocks = []
    for tap_index in range(9):
        row_shift, col_shift = (tap_index // 3, tap_index % 3)
        window = hidden_pad[
            row_shift : row_shift + row_count, col_shift : col_shift + col_count
        ].reshape(row_count * col_count, channels)
        blocks.append(jnp.dot(grad_flat, window, preferred_element_type=jnp.float32))
    return jnp.concatenate(blocks, axis=1)


def per_device(
    latents,
    conv_weight,
    conv_bias,
    out_weight,
    row_table,
    patch_weight,
    pos_embed,
    proj_weight,
    text_embed,
):
    channels = latents.shape[-1]
    row_count = 2 * latents.shape[1]
    width_px = 2 * latents.shape[2]
    height = row_count * lax.axis_size("slab")
    first_row = lax.axis_index("slab") * row_count
    with_rims = with_halo(latents[0], (("slab", 0),), 1)
    upsampled = upsample(with_rims)
    conv_input = column_pad(upsampled[1:-1])
    conv_sum = conv_hidden(conv_input, conv_weight, row_count, width_px) + conv_bias
    hidden = jax.nn.silu(conv_sum).astype(jnp.bfloat16).reshape(row_count, width_px, channels)
    hidden_rows = with_halo(hidden, (("slab", 0),), 1)
    hidden_pad = column_pad(hidden_rows)
    decoded = (
        conv_image(hidden_pad, out_weight, row_count, width_px)
        .astype(jnp.bfloat16)
        .reshape(3, row_count, width_px)
    )
    column_pick = jnp.arange(IMG, dtype=jnp.int32) * width_px // IMG
    column_float = (jnp.arange(width_px, dtype=jnp.int32)[:, None] == column_pick[None, :]).astype(
        jnp.float32
    )
    weights = row_weights(row_table[0], height)
    gathered = lax.all_gather(decoded, "slab", axis=1, tiled=True)
    rows_first = jnp.einsum(
        "ih,chw->ciw", weights, gathered.astype(jnp.float32), precision=lax.Precision.HIGHEST
    )
    crop = jnp.einsum("ciw,wj->cij", rows_first, column_float, precision=lax.Precision.HIGHEST)
    reward, pullback = jax.vjp(
        lambda crop_input: clip_reward(
            crop_input, patch_weight, pos_embed, proj_weight, text_embed
        ),
        crop,
    )
    crop_grad = pullback(jnp.float32(-loss_scale))[0]
    own_weights = lax.dynamic_slice_in_dim(weights, first_row, row_count, 1)
    rows_grad = jnp.einsum("ir,cij->crj", own_weights, crop_grad, precision=lax.Precision.HIGHEST)
    image_grad = jnp.einsum("crj,wj->crw", rows_grad, column_float, precision=lax.Precision.HIGHEST)
    grad_rounded = image_grad.astype(jnp.bfloat16)
    grad_rows = with_halo(grad_rounded, (("slab", 1),), 1)
    grad_pad = jnp.pad(grad_rows, ((0, 0), (0, 0), (1, 1)))
    hidden_grad = image_grad_to_hidden(grad_pad, out_weight, row_count, width_px)
    gate_value = jax.nn.sigmoid(conv_sum)
    conv_grad = (hidden_grad * gate_value * (1.0 + conv_sum * (1.0 - gate_value))).astype(
        jnp.bfloat16
    )
    kernel_local = kernel_grad(conv_input, conv_grad, row_count, width_px)
    out_local = out_kernel_grad(
        grad_rounded.reshape(3, row_count * width_px), hidden_pad, row_count, width_px
    )
    kernel_share = lax.psum_scatter(kernel_local, "slab", scatter_dimension=0, tiled=True)
    kernel_part = lax.psum(kernel_share, "frame")
    out_total = lax.psum(out_local, ("frame", "slab"))
    return (reward.reshape(1), kernel_part, out_total)


def solution(mesh):
    return jax.shard_map(
        per_device,
        mesh=mesh,
        in_specs=(
            P("frame", "slab", None, None),
            P(),
            P(),
            P(),
            P("frame", None),
            P(),
            P(),
            P(),
            P(),
        ),
        out_specs=(P("frame"), P("slab", None), P()),
        check_vma=False,
    )
```

profile of v0, /device:TPU:1, one launch (start us, length us, event | category | flops | bytes accessed | tf_op | source)
XLA Modules:
  0.0 589.0 jit_solution(17479248838488643295)
XLA Ops:
  3.0 5.3 collective-permute-start
  16.2 3.0 slice.228
  19.1 4.6 pad_slice_fusion
  24.8 2.0 reshape.248
  27.9 2.0 reshape.254
  30.0 1.5 fusion.41
  38.2 1.4 multiply_convert_fusion
  41.7 4.3 collective-permute-start.2
  48.0 1.9 collective-permute-done.2
  50.6 1.3 fusion.24
  55.3 132.8 %all_gather.3 = bf16[3,256,256]{2,0,1:T(4,128)(2,1)S(1)} all-gather(bf16[3,4,256]{2,0,1:T(4,128)(2,1)S(1)} %bitcast.218), channel_id=1, replica_groups=mesh['frame'=4,'slab'=64] {'slab'}, dimensions={1}, use_global_device_ids=true | all-gather | bytes 399360 | tf_op jit(solution)/shard_map/all_gather | solution.py:176
  188.6 1.4 fusion.31
  190.0 5.5 reshape.266
  195.6 7.8 %copy.35 = f32[16,16,3,14,14]{1,0,4,3,2:T(8,128)} copy(f32[16,16,3,14,14]{4,1,3,0,2:T(8,128)} %bitcast.185) | data formatting | bytes 1204224 | tf_op jit(solution)/shard_map/jvp()/transpose | solution.py:34
  203.4 4.7 reshape.267
  208.0 3.7 fusion.101
  219.3 2.1 convolution_reduce_fusion
  224.1 1.6 multiply_reduce_fusion
  226.1 3.1 fusion.5
  229.3 3.7 reshape.269
  233.0 7.5 %copy.36 = f32[16,16,3,14,14]{4,1,3,0,2:T(8,128)} copy(f32[16,16,3,14,14]{1,0,4,3,2:T(8,128)} %reshape.269) | data formatting | bytes 1204224 | tf_op jit(solution)/shard_map/transpose(jvp())/reshape | solution.py:35
  240.4 4.7 reshape.270
  248.1 4.0 collective-permute-start.4
  267.9 142.1 %fusion = f32[40,256]{1,0:T(8,128)S(1)} fusion(f32[2304,256]{1,0:T(8,128)} %convolution_dynamic-update-slice_fusion), kind=kCustom, calls=%all-reduce-scatter | all-reduce-scatter fusion | flops 655361 | bytes 2401280
  413.8 1.9 collective-permute-start.10
  415.7 1.9 collective-permute-start.9
  417.6 1.9 collective-permute-start.8
  419.5 1.9 collective-permute-start.7
  422.0 2.5 collective-permute-start.6
  425.4 142.9 %psum.15 = f32[3,2304]{1,0:T(4,128)} all-reduce(f32[3,2304]{1,0:T(4,128)S(1)} %fusion.11), channel_id=1, replica_groups=mesh['frame'=4,'slab'=64] {'frame','slab'}, use_global_device_ids=true, to_apply=%region_14.15 | all-reduce | flops 6912 | bytes 55296 | tf_op jit(solution)/shard_map/psum | solution.py:205
  568.4 5.1 concatenate.50
  573.5 14.4 %psum.14 = f32[36,256]{1,0:T(8,128)} all-reduce(f32[36,256]{1,0:T(8,128)S(1)} %constant_dynamic-slice_fusion), channel_id=1, replica_groups=mesh['frame'=4,'slab'=64] {'frame'}, use_global_device_ids=true, to_apply=%region_13.14 | all-reduce | flops 9216 | bytes 73728 | tf_op jit(solution)/shard_map/psum | solution.py:204
  (196 shorter events, 55.8 us)
Async XLA Ops:
  0.6 214.8 %copy-start = (bf16[1280,1024]{1,0:T(8,128)(2,1)S(1)}, bf16[1280,1024]{1,0:T(8,128)(2,1)}, u32[]{:S(2)}) copy-start(bf16[1280,1024]{1,0:T(8,128)(2,1)} %param.16) | copy-start | bytes 7864324
  0.6 12.4 %copy-start.25 = (bf16[1,2,128,256]{3,2,1,0:T(8,128)(2,1)S(1)}, bf16[1,2,128,256]{3,2,1,0:T(8,128)(2,1)}, u32[]{:S(2)}) copy-start(bf16[1,2,128,256]{3,2,1,0:T(8,128)(2,1)} %param.9) | copy-start | bytes 393220
  1.7 11.3 %collective-permute-start.1 = (bf16[1,128,256]{2,1,0:T(8,128)(2,1)S(1)}, bf16[1,128,256]{2,1,0:T(8,128)(2,1)S(1)}, u32[]{:S(2)}, u32[]{:S(2)}) collective-permute-start(bf16[1,128,256]{2,1,0:T(8,128)(2,1)S(1)} %get-tuple-element.25), channel_id=1, source_target_pairs={{1,0},{2,1},{3,2},{4,3},{5,4},{6,5},{7,6},{8,7},{9,8},{10,9},{11,1... | collective-permute-start | bytes 196616 | tf_op jit(solution)/shard_map/ppermute | solution.py:22
  3.0 10.1 %collective-permute-start = (bf16[1,128,256]{2,1,0:T(8,128)(2,1)S(1)}, bf16[1,128,256]{2,1,0:T(8,128)(2,1)}, u32[]{:S(2)}, u32[]{:S(2)}) collective-permute-start(bf16[1,128,256]{2,1,0:T(8,128)(2,1)S(1)} %get-tuple-element.24), channel_id=1, source_target_pairs={{0,1},{1,2},{2,3},{3,4},{4,5},{5,6},{6,7},{7,8},{8,9},{9,10},{10,1... | collective-permute-start | bytes 196616 | tf_op jit(solution)/shard_map/ppermute | solution.py:19
  13.0 21.0 %copy-start.10 = (bf16[1024,256]{1,0:T(8,128)(2,1)}, bf16[1024,256]{1,0:T(8,128)(2,1)S(1)}, u32[]{:S(2)}) copy-start(bf16[1024,256]{1,0:T(8,128)(2,1)S(1)} %reshape.251) | copy-start | bytes 1572868
  19.1 4.6 copy-start.26
  38.2 7.8 %copy-start.37 = (s32[1,224]{1,0:T(1,128)S(1)}, s32[1,224]{1,0:T(1,128)}, u32[]{:S(2)}) copy-start(s32[1,224]{1,0:T(1,128)} %param.13) | copy-start | bytes 2692
  38.2 8.6 %copy-start.38 = (u32[256]{0:T(256)S(1)}, u32[256]{0:T(256)}, u32[]{:S(2)}) copy-start(u32[256]{0:T(256)} %constant.84) | copy-start | bytes 3076
  39.6 10.4 %copy-start.4 = (bf16[1024,256]{1,0:T(8,128)(2,1)}, bf16[1024,256]{1,0:T(8,128)(2,1)S(1)}, u32[]{:S(2)}) copy-start(bf16[1024,256]{1,0:T(8,128)(2,1)S(1)} %get-tuple-element.40) | copy-start | bytes 1572868
  40.4 7.6 %collective-permute-start.3 = (bf16[1,256,256]{2,1,0:T(8,128)(2,1)}, bf16[1,256,256]{2,1,0:T(8,128)(2,1)S(1)}, u32[]{:S(2)}, u32[]{:S(2)}) collective-permute-start(bf16[1,256,256]{2,1,0:T(8,128)(2,1)} %get-tuple-element.21), channel_id=1, source_target_pairs={{1,0},{2,1},{3,2},{4,3},{5,4},{6,5},{7,6},{8,7},{9,8},{10,9},{11,1... | collective-permute-start | bytes 393224 | tf_op jit(solution)/shard_map/ppermute | solution.py:22
  41.7 8.3 %collective-permute-start.2 = (bf16[1,256,256]{2,1,0:T(8,128)(2,1)}, bf16[1,256,256]{2,1,0:T(8,128)(2,1)S(1)}, u32[]{:S(2)}, u32[]{:S(2)}) collective-permute-start(bf16[1,256,256]{2,1,0:T(8,128)(2,1)} %get-tuple-element.20), channel_id=1, source_target_pairs={{0,1},{1,2},{2,3},{3,4},{4,5},{5,6},{6,7},{7,8},{8,9},{9,10},{10,1... | collective-permute-start | bytes 393224 | tf_op jit(solution)/shard_map/ppermute | solution.py:19
  48.0 1.9 copy-start.28
  221.5 4.2 copy-start.3
  245.1 7.0 %copy-start.9 = (bf16[4,256,256]{2,1,0:T(8,128)(2,1)S(1)}, bf16[4,256,256]{2,1,0:T(8,128)(2,1)}, u32[]{:S(2)}) copy-start(bf16[4,256,256]{2,1,0:T(8,128)(2,1)} %copy-done.8) | copy-start | bytes 1572868
  246.6 6.1 %copy-start.6 = (bf16[1024,256]{1,0:T(8,128)(2,1)S(1)}, bf16[1024,256]{1,0:T(8,128)(2,1)}, u32[]{:S(2)}) copy-start(bf16[1024,256]{1,0:T(8,128)(2,1)} %copy-done.4) | copy-start | bytes 1572868
  246.8 6.6 %collective-permute-start.5 = (bf16[3,1,256]{2,1,0:T(2,128)(2,1)S(1)}, bf16[3,1,256]{2,1,0:T(2,128)(2,1)S(1)}, u32[]{:S(2)}, u32[]{:S(2)}) collective-permute-start(bf16[3,1,256]{2,1,0:T(2,128)(2,1)S(1)} %get-tuple-element.35), channel_id=1, source_target_pairs={{1,0},{2,1},{3,2},{4,3},{5,4},{6,5},{7,6},{8,7},{9,8},{10,9},{11,1... | collective-permute-start | bytes 4616 | tf_op jit(solution)/shard_map/ppermute | solution.py:22
  248.1 5.3 collective-permute-start.4
  258.5 2.1 copy-start.20
  259.5 2.1 copy-start.18
  260.6 2.1 copy-start.11
  261.6 2.1 copy-start.16
  262.6 2.1 copy-start.14
  263.7 2.1 copy-start.22
  264.8 2.1 copy-start.33
  267.9 320.0 %copy-start.1 = (bf16[1280,1024]{1,0:T(8,128)(2,1)S(1)}, bf16[1280,1024]{1,0:T(8,128)(2,1)}, u32[]{:S(2)}) copy-start(bf16[1280,1024]{1,0:T(8,128)(2,1)} %param.16) | copy-start | bytes 7864324
  410.0 11.4 %collective-permute-start.11 = (f32[40,256]{1,0:T(8,128)S(1)}, f32[40,256]{1,0:T(8,128)S(1)}, u32[]{:S(2)}, u32[]{:S(2)}) collective-permute-start(f32[40,256]{1,0:T(8,128)S(1)} %fusion), channel_id=1, source_target_pairs={{0,6},{1,7},{2,8},{3,9},{4,10},{5,11},{6,12},{7,13},{8,14},{9,15},... | collective-permute-start | bytes 122888
  411.3 8.2 %collective-permute-start.12 = (f32[12,256]{1,0:T(8,128)S(1)}, f32[12,256]{1,0:T(8,128)S(1)}, u32[]{:S(2)}, u32[]{:S(2)}) collective-permute-start(f32[12,256]{1,0:T(8,128)S(1)} %slice.298), channel_id=1, source_target_pairs={{0,7},{1,8},{2,9},{3,10},{4,11},{5,12},{6,13},{7,14},{8,15},{9,16}... | collective-permute-start | bytes 36872
  413.8 154.5 %collective-permute-start.10 = (f32[40,256]{1,0:T(8,128)S(1)}, f32[40,256]{1,0:T(8,128)}, u32[]{:S(2)}, u32[]{:S(2)}) collective-permute-start(f32[40,256]{1,0:T(8,128)S(1)} %fusion), channel_id=1, source_target_pairs={{0,5},{1,6},{2,7},{3,8},{4,9},{5,10},{6,11},{7,12},{8,13},{9,14},{... | collective-permute-start | bytes 122888
  415.7 152.6 %collective-permute-start.9 = (f32[40,256]{1,0:T(8,128)S(1)}, f32[40,256]{1,0:T(8,128)}, u32[]{:S(2)}, u32[]{:S(2)}) collective-permute-start(f32[40,256]{1,0:T(8,128)S(1)} %fusion), channel_id=1, source_target_pairs={{0,4},{1,5},{2,6},{3,7},{4,8},{5,9},{6,10},{7,11},{8,12},{9,13},{1... | collective-permute-start | bytes 122888
  417.6 150.7 %collective-permute-start.8 = (f32[40,256]{1,0:T(8,128)S(1)}, f32[40,256]{1,0:T(8,128)}, u32[]{:S(2)}, u32[]{:S(2)}) collective-permute-start(f32[40,256]{1,0:T(8,128)S(1)} %fusion), channel_id=1, source_target_pairs={{0,3},{1,4},{2,5},{3,6},{4,7},{5,8},{6,9},{7,10},{8,11},{9,12},{10... | collective-permute-start | bytes 122888
  419.5 148.9 %collective-permute-start.7 = (f32[40,256]{1,0:T(8,128)S(1)}, f32[40,256]{1,0:T(8,128)}, u32[]{:S(2)}, u32[]{:S(2)}) collective-permute-start(f32[40,256]{1,0:T(8,128)S(1)} %fusion), channel_id=1, source_target_pairs={{0,2},{1,3},{2,4},{3,5},{4,6},{5,7},{6,8},{7,9},{8,10},{9,11},{10,... | collective-permute-start | bytes 122888
  422.0 146.4 %collective-permute-start.6 = (f32[40,256]{1,0:T(8,128)S(1)}, f32[40,256]{1,0:T(8,128)}, u32[]{:S(2)}, u32[]{:S(2)}) collective-permute-start(f32[40,256]{1,0:T(8,128)S(1)} %fusion), channel_id=1, source_target_pairs={{0,1},{1,2},{2,3},{3,4},{4,5},{5,6},{6,7},{7,8},{8,9},{9,10},{10,1... | collective-permute-start | bytes 122888
  (22 other events, 24.2 us)
where the time goes:
time: 591 us; the launch traced here: 589 us
  blocking collectives  432 us (73%)
  local copies, waits for them, and re-layouts  70.3 us (12%)
  matrix products  36.2 us (6%)
  starting transfers between devices  30.1 us (5%)
  other arithmetic  9.65 us (2%)
  between operations  8.68 us (1%)
    psum x1, blocking collectives, per_device(): out_total = lax.psum(out_local, ('frame', 'slab'))  143 us
    unnamed x1, blocking collectives  142 us
    all_gather x1, blocking collectives, per_device(): gathered = lax.all_gather(decoded, 'slab', axis=1, tiled=True)  133 us
    reshape x3, local copies, waits for them, and re-layouts, clip_reward(): patches = patches.reshape(grid_side * grid_side, 3 * PATCH * PATCH)  15.8 us
    psum x1, blocking collectives, per_device(): kernel_part = lax.psum(kernel_share, 'frame')  14.4 us
    unnamed x96, local copies, waits for them, and re-layouts  14.3 us
    ppermute x3, starting transfers between devices, with_halo(): lax.ppermute(lax.slice_in_dim(block, block.shape[dim] - width, None, axis...  13.6 us
    unnamed x7, starting transfers between devices  12.6 us
  transfers between devices with their start and end apart: 13, of which 1 were waited for; matrix products, arithmetic and copies ran while one was open for 1% of the time, Pallas kernels for 0%

commit v1 on v0

v1 whole, which is shorter than its diff:
```python
import jax
import jax.numpy as jnp
from jax import lax
from jax.experimental import pallas as pl
from jax.experimental.pallas import tpu as pltpu
from jax.sharding import PartitionSpec as P

MESH = pl.DeviceIdType.MESH
F32 = jnp.float32
BF16 = jnp.bfloat16

C = 256
CW = 1280
EMB = 1024
IMG = 224
PATCH = 14
WL = 128
N_SLAB = 64
GROUPS = 16
KP = 14 * 64
LOSS_SCALE = 256.0
EPS = 1e-05


def dot_nn(a, b):
    return lax.dot_general(a, b, (((1,), (0,)), ((), ())), preferred_element_type=F32)


def dot_nt(a, b):
    return lax.dot_general(a, b, (((1,), (1,)), ((), ())), preferred_element_type=F32)


def dot_tn(a, b):
    return lax.dot_general(a, b, (((0,), (0,)), ((), ())), preferred_element_type=F32)


def iota(shape, dim):
    return lax.broadcasted_iota(jnp.int32, shape, dim)


def split2(v):
    hi = v.astype(BF16)
    lo = (v - hi.astype(F32)).astype(BF16)
    return hi, lo


def lat_row(r6, a):
    return (r6 - 1 + a - 1) // 2 + 1


def patch_column(c14):
    c16 = c14 * 8 // 7
    return c16 % 2, c16 // 2


def kernel(
    lat_hbm, cw_hbm, bias_ref, ow_ref, table_ref, pw_hbm, pos_hbm, proj_hbm, text_ref,
    reward_ref, gconv_ref, gout_ref,
    lat4, wb, lcat, zbuf, hbuf, gate, wd32, wo32, pw, pwp, pos, proj,
    dec, dall, ct, gt, ybuf, psend, precv, igs, latt,
    g32, gbf, gcr, xbf, x32, xr, zbf, z32, zr, yb, yr,
    go2, gocr, goz, gozr, gox, goxr,
    loc_sem, halo_ss, halo_rs, gat_ss, gat_rs, pool_ss, pool_rs,
    c_ss, c_rs, x_ss, x_rs, z_ss, z_rs, y_ss, y_rs,
):
    f = lax.axis_index("frame")
    s = lax.axis_index("slab")
    y_hi, core = f // 2, f % 2
    x, z, y_lo = s // 16, (s % 16) // 2, s % 2
    p, q = s // 4, s % 4
    low_half = q < 2
    base = jnp.where(low_half, 4 * p - 4, 4 * p)
    p2 = jnp.where(low_half, p - 1, p + 1)
    p2c = jnp.clip(p2, 0, GROUPS - 1)

    loads = []

    def load(src, dst):
        copy = pltpu.make_async_copy(src, dst, loc_sem.at[len(loads)])
        copy.start()
        loads.append(copy)
        return copy

    lat_load = load(lat_hbm.at[0], lat4.at[pl.ds(1, 2)])
    w_loads = []
    for a in range(3):
        for b in range(3):
            t = 3 * a + b
            w_loads.append(
                load(cw_hbm.at[pl.ds(t * C, C)], wb.at[b, pl.ds(a * C, C)])
            )
    pw_load = load(pw_hbm, pw)
    pos_loads = [
        load(pos_hbm.at[pl.ds(pl.multiple_of(16 * p, 16), 16)], pos.at[pl.ds(0, 16)]),
        load(pos_hbm.at[pl.ds(pl.multiple_of(16 * p2c, 16), 16)], pos.at[pl.ds(16, 16)]),
    ]
    proj_load = load(proj_hbm, proj)

    dall[...] = jnp.zeros_like(dall)
    lat4[0] = jnp.zeros((WL, C), BF16)
    lat4[3] = jnp.zeros((WL, C), BF16)

    barrier = pltpu.get_barrier_semaphore()

    def greet(cond, fd, sd):
        def go():
            pl.semaphore_signal(barrier, inc=1, device_id=(fd, sd), device_id_type=MESH)

        if cond is None:
            go()
        else:
            pl.when(cond)(go)

    greet(s > 0, f, s - 1)
    greet(s < N_SLAB - 1, f, s + 1)
    for d in range(1, 4):
        greet(None, f, 4 * p + (q + d) % 4)
    for v in range(4):
        greet((q == 0) & (p > 0), f, 4 * p - 4 + v)
        greet((q == 3) & (p < GROUPS - 1), f, 4 * p + 4 + v)
    greet((q < 3) & (p < GROUPS - 1), f, 4 * p + 4)
    greet((q == 3) & (p < GROUPS - 2), f, 4 * p + 8)
    for d in range(1, GROUPS):
        greet(None, f, 4 * ((p + d) % GROUPS) + q)
    for d in range(1, 4):
        greet(None, f, ((x + d) % 4) * 16 + z * 2 + y_lo)
    for d in range(1, 8):
        greet(None, f, x * 16 + ((z + d) % 8) * 2 + y_lo)
    yc = y_hi * 4 + y_lo * 2 + core

    def yc_device(idx):
        return (idx // 4) * 2 + idx % 2, x * 16 + z * 2 + (idx // 2) % 2

    for d in range(1, 8):
        greet(None, *yc_device((yc + d) % 8))

    def one(cond):
        return jnp.where(cond, 1, 0)

    expected = (
        one(s > 0) + one(s < N_SLAB - 1)
        + 3 + one(p < GROUPS - 1) + one(p > 0)
        + one((q == 0) & (p > 0)) * 3 + one((q == 0) & (p > 1))
        + 15 + 3 + 7 + 7
    )

    wd32[...] = jnp.zeros_like(wd32)
    wo32[...] = jnp.zeros_like(wo32)
    for a in range(3):
        for b in range(3):
            t = 3 * a + b
            tap = ow_ref[:, t * C:(t + 1) * C].astype(F32)
            wo32[b * 16 + (2 - a) * 4:b * 16 + (2 - a) * 4 + 3, :] = tap
            for r in range(4):
                wd32[b * 16 + r * 4:b * 16 + r * 4 + 3, (r + a) * C:(r + a + 1) * C] = tap

    pl.semaphore_wait(barrier, expected)

    sends = []

    def remote(src, dst, ssem, rsem, fd, sd):
        return pltpu.make_async_remote_copy(
            src_ref=src, dst_ref=dst, send_sem=ssem, recv_sem=rsem,
            device_id=(fd, sd), device_id_type=MESH,
        )

    def guard(cond, action):
        if cond is None:
            action()
        else:
            pl.when(cond)(action)

    def send(cond, *what):
        copy = remote(*what)
        guard(cond, copy.start)
        sends.append((cond, copy))
        return copy

    up = send(s > 0, lat_hbm.at[0, 0], lat4.at[3], halo_ss.at[0], halo_rs.at[1], f, s - 1)
    down = send(
        s < N_SLAB - 1, lat_hbm.at[0, 1], lat4.at[0], halo_ss.at[1], halo_rs.at[0], f, s + 1
    )

    bias = bias_ref[...]
    first = iota((WL, C), 0) == 0
    last = iota((WL, C), 0) == WL - 1

    def conv_rows(rows):
        count = len(rows)
        for n, r6 in enumerate(rows):
            for a in range(3):
                lcat[n * WL:(n + 1) * WL, a * C:(a + 1) * C] = lat4[lat_row(r6, a)]
        for b in range(3):
            zbuf[b, 0:count * WL] = dot_nn(lcat[0:count * WL, :], wb[b])
        for n, r6 in enumerate(rows):
            here = slice(n * WL, (n + 1) * WL)
            z0, z1, z2 = zbuf[0, here], zbuf[1, here], zbuf[2, here]
            before = jnp.where(first, 0.0, pltpu.roll(z0, 1, 0))
            after = jnp.where(last, 0.0, pltpu.roll(z2, WL - 1, 0))
            for pc, total in ((0, before + z1 + z2), (1, z0 + z1 + after)):
                total = total + bias
                hidden = total / (1.0 + jnp.exp(-total))
                if r6 == 0:
                    hidden = jnp.where(s > 0, hidden, 0.0)
                elif r6 == 5:
                    hidden = jnp.where(s < N_SLAB - 1, hidden, 0.0)
                else:
                    gate[pc * WL:(pc + 1) * WL, (r6 - 1) * C:r6 * C] = total
                hbuf[pc * WL:(pc + 1) * WL, r6 * C:(r6 + 1) * C] = hidden.astype(BF16)

    lat_load.wait()
    for copy in w_loads:
        copy.wait()
    conv_rows([2, 3])

    guard(s < N_SLAB - 1, up.wait_recv)
    guard(s > 0, down.wait_recv)
    conv_rows([0, 1, 4, 5])

    res = dot_nt(wd32[...].astype(BF16), hbuf[...])
    even, odd = res[:, 0:WL], res[:, WL:2 * WL]
    left = iota((16, WL), 1) == 0
    right = iota((16, WL), 1) == WL - 1
    dec_even = jnp.where(left, 0.0, pltpu.roll(odd[0:16], 1, 1)) + even[16:32] + odd[32:48]
    dec_odd = even[0:16] + odd[16:32] + jnp.where(right, 0.0, pltpu.roll(even[32:48], WL - 1, 1))
    decoded = jnp.concatenate([dec_even, dec_odd], axis=1).astype(BF16)
    dec[...] = decoded
    dall[jnp.where(low_half, q + 4, q)] = decoded

    def gather_send(n, cond, target, slot):
        send(cond, dec, dall.at[slot], gat_ss.at[n], gat_rs.at[slot], f, target)

    for d in range(1, 4):
        qd = (q + d) % 4
        gather_send(d - 1, None, 4 * p + qd, jnp.where(qd < 2, q + 4, q))
    gather_send(3, p < GROUPS - 1, 4 * p + 4, q)
    gather_send(4, p > 0, 4 * p - 1, q + 4)
    gather_send(5, (q == 0) & (p > 0), 4 * p - 4, 8)
    gather_send(6, (q == 0) & (p > 0), 4 * p - 3, 8)
    gather_send(7, (q == 0) & (p > 0), 4 * p - 2, 4)
    gather_send(8, (q == 0) & (p > 1), 4 * p - 5, 8)

    rk = iota((128, 1), 0)
    g = rk & 63
    colour = one(g >= 14) + one(g >= 28)
    ig = jnp.where(rk < 64, p, p2) * PATCH + g - 14 * colour
    valid = (g < 42) & (ig >= 0) & (ig < IMG)
    table = table_ref[...].astype(F32)
    cols = iota((128, IMG), 1)
    lo = jnp.sum(jnp.where(cols == ig, table, 0.0), axis=1, keepdims=True)
    nxt = jnp.sum(jnp.where(cols == ig + 1, table, 0.0), axis=1, keepdims=True)
    nxt = nxt + jnp.where(ig == IMG - 1, 256.0, 0.0)
    hi = jnp.maximum(nxt, lo + 1.0)
    inv = 1.0 / (hi - lo)
    lane = iota((128, 144), 1)
    row = (4 * base + (lane >> 2)).astype(F32)
    inside = valid & ((lane & 3) == colour) & (row >= lo) & (row < hi)
    pick = jnp.where(inside, 1.0, 0.0).astype(BF16)
    lane = iota((128, 128), 1)
    row = (4 * s - 1 + (lane >> 2)).astype(F32)
    inside = valid & ((lane & 3) == colour) & (row >= lo) & (row < hi) & (lane < 24)
    both = jnp.where(lane == 32, inv, jnp.where(inside, 1.0, 0.0)).T
    back = both[0:32].astype(BF16)
    back = jnp.concatenate([back, back], axis=1)
    inv_row = both[32:33]

    pw_load.wait()
    prow = iota((KP, 588), 0)
    pg = prow & 63
    order = jnp.where(
        (pg < 42) & (iota((KP, 588), 1) == 14 * pg + 2 * (prow >> 7) + ((prow >> 6) & 1)), 1.0, 0.0
    ).astype(BF16)
    for n in range(CW // 256):
        cut = slice(n * 256, (n + 1) * 256)
        pwp[:, cut] = dot_nn(order, pw[:, cut]).astype(BF16)

    def gather_wait(slot, cond, source):
        copy = remote(dec, dall.at[slot], gat_ss.at[0], gat_rs.at[slot], f, source)
        pl.when(cond)(copy.wait_recv)

    more = p < GROUPS - 1
    for v in range(4):
        gather_wait(
            v, (low_half & (q == 0) & (p > 0)) | ((q >= 2) & (q != v)),
            jnp.where(low_half, 4 * p - 4 + v, 4 * p + v),
        )
        if v == 0:
            cond = (low_half & (q != v)) | ((q >= 2) & more)
        else:
            cond = (low_half & (q != v)) | ((q == 3) & more)
        gather_wait(v + 4, cond, jnp.where(low_half, 4 * p + v, 4 * p + 4 + v))
    gather_wait(
        8, (low_half & more) | ((q == 3) & (p < GROUPS - 2)),
        jnp.where(low_half, 4 * p + 4, 4 * p + 8),
    )

    crop = dot_nn(pick, dall[...].reshape(144, 256)) * inv
    ct[...] = crop.T
    lane16 = iota((16, 128), 1) < 64
    parts0, parts1 = [], []
    for n in range(7):
        pair = []
        for c14 in (2 * n, 2 * n + 1):
            pc, pj = patch_column(c14)
            pair.append(ct[pl.ds(pc * WL + pj, 16, stride=8), :])
        parts0.append(jnp.where(lane16, pair[0], pltpu.roll(pair[1], 64, 1)))
        parts1.append(jnp.where(lane16, pltpu.roll(pair[0], 64, 1), pair[1]))
    patches = jnp.concatenate(
        [jnp.concatenate(parts0, axis=1), jnp.concatenate(parts1, axis=1)], axis=0
    )
    for copy in pos_loads:
        copy.wait()
    emb = dot_nn(jnp.concatenate(split2(patches), axis=0), pwp[...])
    emb = emb[0:32] + emb[32:64] + pos[...].astype(F32)
    centred = emb - jnp.mean(emb, axis=1, keepdims=True)
    sigma = jnp.sqrt(jnp.mean(centred * centred, axis=1, keepdims=True) + EPS)
    normed = centred / sigma
    ybuf[...] = normed
    gsum = jnp.sum(normed[0:16], axis=0, keepdims=True)
    psend[...] = gsum
    precv[p] = gsum

    for d in range(1, GROUPS):
        send(
            None, psend, precv.at[p], pool_ss.at[d], pool_rs.at[p],
            f, 4 * ((p + d) % GROUPS) + q,
        )

    for n in range(4):
        cut = slice(n * C, (n + 1) * C)
        total = gate[:, cut]
        sig = 1.0 / (1.0 + jnp.exp(-total))
        gate[:, cut] = sig * (1.0 + total * (1.0 - sig))
    for n in range(4):
        latt[:, n * WL:(n + 1) * WL] = lat4[n].astype(F32).T.astype(BF16)
    text = text_ref[...]
    text2 = jnp.sum(text * text, axis=1, keepdims=True) + 1e-06
    gt[...] = jnp.zeros_like(gt)

    for d in range(1, GROUPS):
        pd = (p + d) % GROUPS
        remote(
            psend, precv.at[pd], pool_ss.at[d], pool_rs.at[pd], f, 4 * pd + q
        ).wait_recv()
    pooled = precv[0]
    for n in range(1, GROUPS):
        pooled = pooled + precv[n]
    pooled = pooled * (1.0 / 256.0)

    proj_load.wait()

    def two_rows(v):
        top = iota((16, v.shape[1]), 0)
        hi_part = v.astype(BF16).astype(F32)
        return jnp.where(top == 0, hi_part, jnp.where(top == 1, v - hi_part, 0.0)).astype(BF16)

    pc_ = pooled - jnp.mean(pooled, axis=1, keepdims=True)
    psigma = jnp.sqrt(jnp.mean(pc_ * pc_, axis=1, keepdims=True) + EPS)
    unit = pc_ / psigma
    projected = jnp.sum(dot_nn(two_rows(unit), proj[...]), axis=0, keepdims=True)
    numer = jnp.sum(projected * text, axis=1, keepdims=True)
    norm2 = jnp.sum(projected * projected, axis=1, keepdims=True) + 1e-06
    scale = 1.0 / jnp.sqrt(norm2 * text2)
    reward = numer * scale
    reward_ref[0] = reward[0, 0]
    dproj = -LOSS_SCALE * (text * scale - projected * (reward / norm2))
    dunit = jnp.sum(dot_nt(two_rows(dproj), proj[...]), axis=0, keepdims=True)

    def norm_back(dy, y, sg):
        m1 = jnp.mean(dy, axis=1, keepdims=True)
        m2 = jnp.mean(dy * y, axis=1, keepdims=True)
        return (dy - m1 - y * m2) / sg

    dpooled = norm_back(dunit, unit, psigma) * (1.0 / 256.0)
    demb = norm_back(dpooled, ybuf[...], sigma)
    dpat = dot_nt(jnp.concatenate(split2(demb), axis=0), pwp[...])
    dpat = dpat[0:32] + dpat[32:64]
    for n in range(7):
        d0 = dpat[0:16, n * 128:(n + 1) * 128]
        d1 = dpat[16:32, n * 128:(n + 1) * 128]
        pair = (
            jnp.where(lane16, d0, pltpu.roll(d1, 64, 1)),
            jnp.where(lane16, pltpu.roll(d0, 64, 1), d1),
        )
        for half in range(2):
            pc, pj = patch_column(2 * n + half)
            gt[pl.ds(pc * WL + pj, 16, stride=8), :] = pair[half]

    grows = jnp.concatenate(split2(gt[...] * inv_row), axis=1)
    image = dot_nt(back, grows).astype(BF16).astype(F32)
    even, odd = image[:, 0:WL], image[:, WL:2 * WL]
    left = iota((32, WL), 1) == 0
    right = iota((32, WL), 1) == WL - 1
    odd_before = jnp.where(left, 0.0, pltpu.roll(odd, 1, 1))
    even_after = jnp.where(right, 0.0, pltpu.roll(even, WL - 1, 1))
    igs[0] = jnp.concatenate([odd, even_after], axis=1)
    igs[1] = image
    igs[2] = jnp.concatenate([odd_before, even], axis=1)

    wout = wo32[...].astype(BF16)
    go = jnp.zeros((48, C), F32)
    cols_of = []
    for r in range(4):
        im = jnp.concatenate([igs[b, 4 * r:4 * r + 16, :] for b in range(3)], axis=0).astype(BF16)
        go = go + dot_nn(im, hbuf[:, (r + 1) * C:(r + 2) * C])
        cg = dot_tn(im, wout) * gate[:, r * C:(r + 1) * C]
        ev, od = cg[0:WL], cg[WL:2 * WL]
        od_before = jnp.where(first, 0.0, pltpu.roll(od, 1, 0))
        ev_after = jnp.where(last, 0.0, pltpu.roll(ev, WL - 1, 0))
        cols_of.append((od + ev_after, ev + od, od_before + ev))

    for b in range(3):
        for half in range(2):
            go2[half, b * 12:(b + 1) * 12, :] = go[b * 16:b * 16 + 12, half * 128:(half + 1) * 128]
    for half in range(2):
        go2[half, 36:40, :] = jnp.zeros((4, 128), F32)

    def put_grad(a, b, value):
        at = (3 * a + b) * C
        for half in range(2):
            part = value[:, half * 128:(half + 1) * 128]
            g32[half, at:at + C, :] = part
            gbf[half, at:at + C, :] = part.astype(BF16)

    for b in range(3):
        u0, u1, u2, u3 = (cols_of[r][b] for r in range(4))
        outer = jnp.concatenate([u0, u1 + u2, u3], axis=0).astype(BF16)
        inner = jnp.concatenate([u0 + u1, u2 + u3], axis=0).astype(BF16)
        put_grad(0, b, dot_nn(latt[:, 0:3 * WL], outer))
        put_grad(1, b, dot_nn(latt[:, WL:3 * WL], inner))
        put_grad(2, b, dot_nn(latt[:, WL:4 * WL], outer))

    fc = y_hi * 2 + 1 - core
    main = send(None, gbf.at[1 - core], gcr, c_ss.at[0], c_rs.at[0], fc, s)
    outk = send(None, go2.at[1 - core], gocr, c_ss.at[1], c_rs.at[1], fc, s)
    outk.wait_recv()
    gsum_z = go2[core] + gocr[...]
    goz[...] = gsum_z
    for d in range(1, 8):
        zd = (z + d) % 8
        send(
            None, goz, gozr.at[z], z_ss.at[0, d], z_rs.at[0, z], f, x * 16 + zd * 2 + y_lo
        )
    main.wait_recv()
    for n in range(4):
        cut = slice(n * 576, (n + 1) * 576)
        total = g32[core, cut, :] + gcr[cut, :].astype(F32)
        x32[n] = total
        xbf[n] = total.astype(BF16)

    for d in range(1, 4):
        xd = (x + d) % 4
        send(
            None, xbf.at[xd], xr.at[x], x_ss.at[0, d], x_rs.at[0, x], f, xd * 16 + z * 2 + y_lo
        )
    gozr[z] = gsum_z
    for d in range(1, 8):
        zd = (z + d) % 8
        remote(
            goz, gozr.at[zd], z_ss.at[0, d], z_rs.at[0, zd], f, x * 16 + zd * 2 + y_lo
        ).wait_recv()
    gsum_x = jnp.sum(gozr[...], axis=0)
    gox[...] = gsum_x
    xr[x] = jnp.zeros((576, 128), BF16)
    for d in range(1, 4):
        xd = (x + d) % 4
        remote(
            xbf.at[xd], xr.at[xd], x_ss.at[0, d], x_rs.at[0, xd], f, xd * 16 + z * 2 + y_lo
        ).wait_recv()
    for n in range(8):
        cut = slice(n * 72, (n + 1) * 72)
        total = x32[x, cut, :]
        for k in range(4):
            total = total + xr[k, cut, :].astype(F32)
        z32[n] = total
        zbf[n] = jnp.concatenate([total, jnp.zeros((8, 128), F32)], axis=0).astype(BF16)

    for d in range(1, 8):
        zd = (z + d) % 8
        send(
            None, zbf.at[zd], zr.at[z], z_ss.at[1, d], z_rs.at[1, z], f, x * 16 + zd * 2 + y_lo
        )
    for d in range(1, 4):
        xd = (x + d) % 4
        send(
            None, gox, goxr.at[x], x_ss.at[1, d], x_rs.at[1, x], f, xd * 16 + z * 2 + y_lo
        )
    goxr[x] = gsum_x
    zr[z] = jnp.zeros((80, 128), BF16)
    for d in range(1, 4):
        xd = (x + d) % 4
        remote(
            gox, goxr.at[xd], x_ss.at[1, d], x_rs.at[1, xd], f, xd * 16 + z * 2 + y_lo
        ).wait_recv()
    gsum_y = jnp.sum(goxr[...], axis=0)
    for d in range(1, 8):
        zd = (z + d) % 8
        remote(
            zbf.at[zd], zr.at[zd], z_ss.at[1, d], z_rs.at[1, zd], f, x * 16 + zd * 2 + y_lo
        ).wait_recv()
    total = z32[z]
    for n in range(8):
        total = total + zr[n, 0:72, :].astype(F32)

    for n in range(2):
        yb[n, 0:36, :] = total[36 * n:36 * n + 36]
        yb[n, 36:40, :] = jnp.zeros((4, 128), F32)
        yb[n, 40:80, :] = gsum_y
    for d in range(1, 8):
        yd = (yc + d) % 8
        send(
            None, yb.at[(yd // 2) % 2], yr.at[yc], y_ss.at[d], y_rs.at[yc], *yc_device(yd)
        )
    yr[yc] = yb[y_lo]
    for d in range(1, 8):
        yd = (yc + d) % 8
        remote(
            yb.at[0], yr.at[yd], y_ss.at[d], y_rs.at[yd], *yc_device(yd)
        ).wait_recv()
    for half in range(2):
        total = (yr[half] + yr[2 + half]) + (yr[4 + half] + yr[6 + half])
        cut = slice(half * 128, (half + 1) * 128)
        gconv_ref[:, cut] = total[0:36]
        for a in range(3):
            for b in range(3):
                at = 40 + b * 12 + (2 - a) * 4
                t = (3 * a + b) * C + half * 128
                gout_ref[:, t:t + 128] = total[at:at + 3]

    for cond, copy in sends:
        guard(cond, copy.wait_send)


def per_device(latents, conv_weight, conv_bias, out_weight, row_table, patch_weight, pos_embed,
               proj_weight, text_embed):
    vmem = pl.BlockSpec(memory_space=pltpu.VMEM)
    hbm = pl.BlockSpec(memory_space=pl.ANY)
    V = pltpu.VMEM
    dma = pltpu.SemaphoreType.DMA
    reward, gconv, gout = pl.pallas_call(
        kernel,
        out_shape=(
            jax.ShapeDtypeStruct((1,), F32),
            jax.ShapeDtypeStruct((36, C), F32),
            jax.ShapeDtypeStruct((3, 9 * C), F32),
        ),
        in_specs=[hbm, hbm, vmem, vmem, vmem, hbm, hbm, hbm, vmem],
        out_specs=(pl.BlockSpec(memory_space=pltpu.SMEM), vmem, vmem),
        scratch_shapes=[
            V((4, WL, C), BF16),
            V((3, 3 * C, C), BF16),
            V((4 * WL, 3 * C), BF16),
            V((3, 4 * WL, C), F32),
            V((2 * WL, 6 * C), BF16),
            V((2 * WL, 4 * C), F32),
            V((48, 6 * C), F32),
            V((48, C), F32),
            V((588, CW), BF16),
            V((KP, CW), BF16),
            V((32, CW), BF16),
            V((CW, EMB), BF16),
            V((16, 256), BF16),
            V((9, 16, 256), BF16),
            V((256, 128), F32),
            V((256, 128), F32),
            V((32, CW), F32),
            V((1, CW), F32),
            V((GROUPS, 1, CW), F32),
            V((3, 32, 256), F32),
            V((C, 4 * WL), BF16),
            V((2, 9 * C, 128), F32),
            V((2, 9 * C, 128), BF16),
            V((9 * C, 128), BF16),
            V((4, 576, 128), BF16),
            V((4, 576, 128), F32),
            V((4, 576, 128), BF16),
            V((8, 80, 128), BF16),
            V((8, 72, 128), F32),
            V((8, 80, 128), BF16),
            V((2, 80, 128), F32),
            V((8, 80, 128), F32),
            V((2, 40, 128), F32),
            V((40, 128), F32),
            V((40, 128), F32),
            V((8, 40, 128), F32),
            V((40, 128), F32),
            V((4, 40, 128), F32),
            dma((14,)), dma((2,)), dma((2,)), dma((9,)), dma((9,)), dma((16,)), dma((16,)),
            dma((2,)), dma((2,)), dma((2, 4)), dma((2, 4)), dma((2, 8)), dma((2, 8)),
            dma((8,)), dma((8,)),
        ],
        compiler_params=pltpu.CompilerParams(
            collective_id=0, has_side_effects=True, vmem_limit_bytes=50 * 1024 * 1024
        ),
    )(
        latents, conv_weight, conv_bias.reshape(1, C), out_weight, row_table, patch_weight,
        pos_embed, proj_weight, text_embed.reshape(1, EMB),
    )
    return reward, gconv, gout


def solution(mesh):
    return jax.shard_map(
        per_device,
        mesh=mesh,
        in_specs=(
            P("frame", "slab", None, None), P(), P(), P(), P("frame", None), P(), P(), P(), P(),
        ),
        out_specs=(P("frame"), P("slab", None), P()),
        check_vma=False,
    )
```

time: 591 us -> 70.7 us (0.12)
  blocking collectives: 432 us -> 0 us
  local copies, waits for them, and re-layouts: 70.3 us -> 8.64 us
  Pallas kernels: 0 us -> 59.3 us
  matrix products: 36.2 us -> 0 us
  starting transfers between devices: 30.1 us -> 0 us
  other arithmetic: 9.65 us -> 0 us
  between operations: 8.68 us -> 2.47 us
    psum x2 -> x0, blocking collectives: 157 us -> none  [the longest x1 143 us: per_device(): out_total = lax.psum(out_local, ('frame', 'slab'))]
    unnamed x1 -> x0, blocking collectives: 142 us -> none
    all_gather x1 -> x0, blocking collectives: 133 us -> none  [per_device(): gathered = lax.all_gather(decoded, 'slab', axis=1, tiled=True)]
    pallas_call x0 -> x1, Pallas kernels: none -> 59.3 us  [per_device(): pl.pallas_call(kernel, out_shape=(jax.ShapeDtypeStruct((1,), F32), jax.Sh...]
    dot_general x53 -> x0, matrix products: 36.2 us -> none  [the longest x9 9.37 us: kernel_grad(): lax.dot_general(window, conv_grad, (((0,), (0,)), ((), ())), preferred_el...]
    reshape x8 -> x0, local copies, waits for them, and re-layouts: 31.4 us -> none  [the longest x3 15.8 us: clip_reward(): patches = patches.reshape(grid_side * grid_side, 3 * PATCH * PATCH)]
    ppermute x6 -> x0, starting transfers between devices: 17.4 us -> none  [the longest x3 13.6 us: with_halo(): lax.ppermute(lax.slice_in_dim(block, block.shape[dim] - width, None, axis...]
    unnamed x7 -> x0, starting transfers between devices: 12.6 us -> none
  transfers between devices with their start and end apart: 13 -> 0, of which waited for: 1 -> 0; matrix products, arithmetic and copies ran while one was open for 1% -> 0% of each run, Pallas kernels for 0% -> 0%
where the time goes in v1:
time: 70.7 us; the launch traced here: 70.4 us
  Pallas kernels  59.3 us (84%)
  local copies, waits for them, and re-layouts  8.64 us (12%)
  between operations  2.47 us (3%)
    pallas_call x1, Pallas kernels, per_device(): pl.pallas_call(kernel, out_shape=(jax.ShapeDtypeStruct((1,), F32), jax.Sh...  59.3 us
    unnamed x18, local copies, waits for them, and re-layouts  8.64 us

profile of v1, /device:TPU:1, one launch (start us, length us, event | category | flops | bytes accessed | tf_op | source)
XLA Modules:
  0.0 70.4 jit_solution(14005082872595577834)
XLA Ops:
  0.6 0.0 copy-start
  0.6 1.4 %copy-done = bf16[588,1280]{1,0:T(8,128)(2,1)S(1)} copy-done((bf16[588,1280]{1,0:T(8,128)(2,1)S(1)}, bf16[588,1280]{1,0:T(8,128)(2,1)}, u32[]{:S(2)}) %copy-start) | copy-done | bytes 1505304
  2.0 0.0 copy-start.1
  2.0 1.3 %copy-done.1 = bf16[2304,256]{1,0:T(8,128)(2,1)S(1)} copy-done((bf16[2304,256]{1,0:T(8,128)(2,1)S(1)}, bf16[2304,256]{1,0:T(8,128)(2,1)}, u32[]{:S(2)}) %copy-start.1) | copy-done | bytes 1179672
  3.3 0.0 copy-start.2
  3.3 1.1 %copy-done.2 = bf16[256,1280]{1,0:T(8,128)(2,1)S(1)} copy-done((bf16[256,1280]{1,0:T(8,128)(2,1)S(1)}, bf16[256,1280]{1,0:T(8,128)(2,1)}, u32[]{:S(2)}) %copy-start.2) | copy-done | bytes 655384
  4.4 0.0 copy-start.3
  4.4 0.9 %copy-done.3 = bf16[1,2,128,256]{3,2,1,0:T(8,128)(2,1)S(1)} copy-done((bf16[1,2,128,256]{3,2,1,0:T(8,128)(2,1)S(1)}, bf16[1,2,128,256]{3,2,1,0:T(8,128)(2,1)}, u32[]{:S(2)}) %copy-start.3) | copy-done | bytes 131096
  5.3 0.0 copy-start.4
  5.3 0.7 %copy-done.4 = bf16[3,2304]{1,0:T(4,128)(2,1)S(1)} copy-done((bf16[3,2304]{1,0:T(4,128)(2,1)S(1)}, bf16[3,2304]{1,0:T(4,128)(2,1)}, u32[]{:S(2)}) %copy-start.4) | copy-done | bytes 13848
  6.0 0.0 copy-start.5
  6.0 0.7 copy-done.5
  6.7 0.0 copy-start.6
  6.7 0.7 copy-done.6
  7.4 0.0 copy-start.7
  7.4 0.7 copy-done.7
  8.1 59.3 %shard_map.112 = (f32[1]{0:T(128)}, f32[36,256]{1,0:T(8,128)S(1)}, f32[3,2304]{1,0:T(4,128)S(1)}) custom-call(bf16[1,2,128,256]{3,2,1,0:T(8,128)(2,1)S(1)} %copy-done.3, bf16[2304,256]{1,0:T(8,128)(2,1)S(1)} %copy-done.1, f32[1,256]{1,0:T(1,128)S(1)} %bitcast.3, bf16[3,2304]{1,0:T(4,128)(2,1)S(1)} %copy-done.4, s32[1,224]{1,0:T(1,128)S(1)} %copy-done.7, ...), custom_call_target="tpu_custom_call" | custom-call | tf_op jit(solution)/shard_map/pallas_call | solution.py:540
  68.0 0.6 copy.16
  68.6 0.6 copy.17
Async XLA Ops:
  0.6 1.4 %copy-start = (bf16[588,1280]{1,0:T(8,128)(2,1)S(1)}, bf16[588,1280]{1,0:T(8,128)(2,1)}, u32[]{:S(2)}) copy-start(bf16[588,1280]{1,0:T(8,128)(2,1)} %pw_hbm.1) | copy-start | bytes 4515844
  2.0 1.3 %copy-start.1 = (bf16[2304,256]{1,0:T(8,128)(2,1)S(1)}, bf16[2304,256]{1,0:T(8,128)(2,1)}, u32[]{:S(2)}) copy-start(bf16[2304,256]{1,0:T(8,128)(2,1)} %cw_hbm.1) | copy-start | bytes 3538948
  3.3 1.1 %copy-start.2 = (bf16[256,1280]{1,0:T(8,128)(2,1)S(1)}, bf16[256,1280]{1,0:T(8,128)(2,1)}, u32[]{:S(2)}) copy-start(bf16[256,1280]{1,0:T(8,128)(2,1)} %pos_hbm.1) | copy-start | bytes 1966084
  4.4 0.9 %copy-start.3 = (bf16[1,2,128,256]{3,2,1,0:T(8,128)(2,1)S(1)}, bf16[1,2,128,256]{3,2,1,0:T(8,128)(2,1)}, u32[]{:S(2)}) copy-start(bf16[1,2,128,256]{3,2,1,0:T(8,128)(2,1)} %lat_hbm.1) | copy-start | bytes 393220
  5.3 0.7 %copy-start.4 = (bf16[3,2304]{1,0:T(4,128)(2,1)S(1)}, bf16[3,2304]{1,0:T(4,128)(2,1)}, u32[]{:S(2)}) copy-start(bf16[3,2304]{1,0:T(4,128)(2,1)} %ow_ref.1) | copy-start | bytes 41476
  6.0 0.7 copy-start.5
  6.7 0.7 copy-start.6
  7.4 0.7 copy-start.7

commit v2 on v1

--- a/solution.py
+++ b/solution.py
@@ -54,12 +54,13 @@
 
 
 def kernel(
-    lat_hbm, cw_hbm, bias_ref, ow_ref, table_ref, pw_hbm, pos_hbm, proj_hbm, text_ref,
+    lat_hbm, cw_hbm, bias_hbm, ow_hbm, table_hbm, pw_hbm, pos_hbm, proj_hbm, text_hbm,
     reward_ref, gconv_ref, gout_ref,
+    bias_ref, ow_ref, table_ref, text_ref,
     lat4, wb, lcat, zbuf, hbuf, gate, wd32, wo32, pw, pwp, pos, proj,
     dec, dall, ct, gt, ybuf, psend, precv, igs, latt,
     g32, gbf, gcr, xbf, x32, xr, zbf, z32, zr, yb, yr,
-    go2, gocr, goz, gozr, gox, goxr,
+    go2, gocr, goz, gozr, gox, goxr, goy, goyr,
     loc_sem, halo_ss, halo_rs, gat_ss, gat_rs, pool_ss, pool_rs,
     c_ss, c_rs, x_ss, x_rs, z_ss, z_rs, y_ss, y_rs,
 ):
@@ -73,6 +74,64 @@
     p2 = jnp.where(low_half, p - 1, p + 1)
     p2c = jnp.clip(p2, 0, GROUPS - 1)
 
+    dall[...] = jnp.zeros_like(dall)
+    lat4[0] = jnp.zeros((WL, C), BF16)
+    lat4[3] = jnp.zeros((WL, C), BF16)
+
+    barrier = pltpu.get_barrier_semaphore()
+
+    def greet(cond, fd, sd):
+        def go():
+            pl.semaphore_signal(barrier, inc=1, device_id=(fd, sd), device_id_type=MESH)
+
+        if cond is None:
+            go()
+        else:
+            pl.when(cond)(go)
+
+    greet(s > 0, f, s - 1)
+    greet(s < N_SLAB - 1, f, s + 1)
+    for d in range(1, 4):
+        greet(None, f, 4 * p + (q + d) % 4)
+    for v in range(4):
+        greet((q == 0) & (p > 0), f, 4 * p - 4 + v)
+        greet((q == 3) & (p < GROUPS - 1), f, 4 * p + 4 + v)
+    greet((q < 3) & (p < GROUPS - 1), f, 4 * p + 4)
+    greet((q == 3) & (p < GROUPS - 2), f, 4 * p + 8)
+    for d in range(1, GROUPS):
+        greet(None, f, 4 * ((p + d) % GROUPS) + q)
+    for d in range(1, 4):
+        greet(None, f, ((x + d) % 4) * 16 + z * 2 + y_lo)
+    for d in range(1, 8):
+        greet(None, f, x * 16 + ((z + d) % 8) * 2 + y_lo)
+    yc = y_hi * 4 + y_lo * 2 + core
+
+    def yc_device(idx):
+        return (idx // 4) * 2 + idx % 2, x * 16 + z * 2 + (idx // 2) % 2
+
+    for d in range(1, 8):
+        greet(None, *yc_device((yc + d) % 8))
+    y = y_hi * 2 + y_lo
+    own_pair = x // 2 == y_hi
+
+    def last_source(slot):
+        if slot < 4:
+            return (slot // 2) * 2, x * 16 + z * 2 + slot % 2
+        return (x // 2) * 2 + 1, (slot - 4) * 16 + z * 2 + y_lo
+
+    for slot in range(4, 8):
+        greet((core == 0) | (y_hi != x // 2) | (x != slot - 4), *last_source(slot))
+
+    def one(cond):
+        return jnp.where(cond, 1, 0)
+
+    expected = (
+        one(s > 0) + one(s < N_SLAB - 1)
+        + 3 + one(p < GROUPS - 1) + one(p > 0)
+        + one((q == 0) & (p > 0)) * 3 + one((q == 0) & (p > 1))
+        + 15 + 3 + 7 + 7 + jnp.where(core == 0, 0, jnp.where(own_pair, 7, 8))
+    )
+
     loads = []
 
     def load(src, dst):
@@ -82,6 +141,10 @@
         return copy
 
     lat_load = load(lat_hbm.at[0], lat4.at[pl.ds(1, 2)])
+    ow_load = load(ow_hbm, ow_ref)
+    bias_load = load(bias_hbm, bias_ref)
+    table_load = load(table_hbm, table_ref)
+    text_load = load(text_hbm, text_ref)
     w_loads = []
     for a in range(3):
         for b in range(3):
@@ -96,56 +159,36 @@
     ]
     proj_load = load(proj_hbm, proj)
 
-    dall[...] = jnp.zeros_like(dall)
-    lat4[0] = jnp.zeros((WL, C), BF16)
-    lat4[3] = jnp.zeros((WL, C), BF16)
-
-    barrier = pltpu.get_barrier_semaphore()
-
-    def greet(cond, fd, sd):
-        def go():
-            pl.semaphore_signal(barrier, inc=1, device_id=(fd, sd), device_id_type=MESH)
-
+    pl.semaphore_wait(barrier, expected)
+
+    sends = []
+
+    def remote(src, dst, ssem, rsem, fd, sd):
+        return pltpu.make_async_remote_copy(
+            src_ref=src, dst_ref=dst, send_sem=ssem, recv_sem=rsem,
+            device_id=(fd, sd), device_id_type=MESH,
+        )
+
+    def guard(cond, action):
         if cond is None:
-            go()
+            action()
         else:
-            pl.when(cond)(go)
-
-    greet(s > 0, f, s - 1)
-    greet(s < N_SLAB - 1, f, s + 1)
-    for d in range(1, 4):
-        greet(None, f, 4 * p + (q + d) % 4)
-    for v in range(4):
-        greet((q == 0) & (p > 0), f, 4 * p - 4 + v)
-        greet((q == 3) & (p < GROUPS - 1), f, 4 * p + 4 + v)
-    greet((q < 3) & (p < GROUPS - 1), f, 4 * p + 4)
-    greet((q == 3) & (p < GROUPS - 2), f, 4 * p + 8)
-    for d in range(1, GROUPS):
-        greet(None, f, 4 * ((p + d) % GROUPS) + q)
-    for d in range(1, 4):
-        greet(None, f, ((x + d) % 4) * 16 + z * 2 + y_lo)
-    for d in range(1, 8):
-        greet(None, f, x * 16 + ((z + d) % 8) * 2 + y_lo)
-    yc = y_hi * 4 + y_lo * 2 + core
-
-    def yc_device(idx):
-        return (idx // 4) * 2 + idx % 2, x * 16 + z * 2 + (idx // 2) % 2
-
-    for d in range(1, 8):
-        greet(None, *yc_device((yc + d) % 8))
-
-    def one(cond):
-        return jnp.where(cond, 1, 0)
-
-    expected = (
-        one(s > 0) + one(s < N_SLAB - 1)
-        + 3 + one(p < GROUPS - 1) + one(p > 0)
-        + one((q == 0) & (p > 0)) * 3 + one((q == 0) & (p > 1))
-        + 15 + 3 + 7 + 7
+            pl.when(cond)(action)
+
+    def send(cond, *what):
+        copy = remote(*what)
+        guard(cond, copy.start)
+        sends.append((cond, copy))
+        return copy
+
+    up = send(s > 0, lat_hbm.at[0, 0], lat4.at[3], halo_ss.at[0], halo_rs.at[1], f, s - 1)
+    down = send(
+        s < N_SLAB - 1, lat_hbm.at[0, 1], lat4.at[0], halo_ss.at[1], halo_rs.at[0], f, s + 1
     )
 
     wd32[...] = jnp.zeros_like(wd32)
     wo32[...] = jnp.zeros_like(wo32)
+    ow_load.wait()
     for a in range(3):
         for b in range(3):
             t = 3 * a + b
@@ -154,33 +197,7 @@
             for r in range(4):
                 wd32[b * 16 + r * 4:b * 16 + r * 4 + 3, (r + a) * C:(r + a + 1) * C] = tap
 
-    pl.semaphore_wait(barrier, expected)
-
-    sends = []
-
-    def remote(src, dst, ssem, rsem, fd, sd):
-        return pltpu.make_async_remote_copy(
-            src_ref=src, dst_ref=dst, send_sem=ssem, recv_sem=rsem,
-            device_id=(fd, sd), device_id_type=MESH,
-        )
-
-    def guard(cond, action):
-        if cond is None:
-            action()
-        else:
-            pl.when(cond)(action)
-
-    def send(cond, *what):
-        copy = remote(*what)
-        guard(cond, copy.start)
-        sends.append((cond, copy))
-        return copy
-
-    up = send(s > 0, lat_hbm.at[0, 0], lat4.at[3], halo_ss.at[0], halo_rs.at[1], f, s - 1)
-    down = send(
-        s < N_SLAB - 1, lat_hbm.at[0, 1], lat4.at[0], halo_ss.at[1], halo_rs.at[0], f, s + 1
-    )
-
+    bias_load.wait()
     bias = bias_ref[...]
     first = iota((WL, C), 0) == 0
     last = iota((WL, C), 0) == WL - 1
@@ -245,6 +262,7 @@
     colour = one(g >= 14) + one(g >= 28)
     ig = jnp.where(rk < 64, p, p2) * PATCH + g - 14 * colour
     valid = (g < 42) & (ig >= 0) & (ig < IMG)
+    table_load.wait()
     table = table_ref[...].astype(F32)
     cols = iota((128, IMG), 1)
     lo = jnp.sum(jnp.where(cols == ig, table, 0.0), axis=1, keepdims=True)
@@ -333,6 +351,7 @@
         gate[:, cut] = sig * (1.0 + total * (1.0 - sig))
     for n in range(4):
         latt[:, n * WL:(n + 1) * WL] = lat4[n].astype(F32).T.astype(BF16)
+    text_load.wait()
     text = text_ref[...]
     text2 = jnp.sum(text * text, axis=1, keepdims=True) + 1e-06
     gt[...] = jnp.zeros_like(gt)
@@ -397,23 +416,28 @@
     igs[1] = image
     igs[2] = jnp.concatenate([odd_before, even], axis=1)
 
-    wout = wo32[...].astype(BF16)
+    ims = []
     go = jnp.zeros((48, C), F32)
-    cols_of = []
     for r in range(4):
         im = jnp.concatenate([igs[b, 4 * r:4 * r + 16, :] for b in range(3)], axis=0).astype(BF16)
+        ims.append(im)
         go = go + dot_nn(im, hbuf[:, (r + 1) * C:(r + 2) * C])
-        cg = dot_tn(im, wout) * gate[:, r * C:(r + 1) * C]
-        ev, od = cg[0:WL], cg[WL:2 * WL]
-        od_before = jnp.where(first, 0.0, pltpu.roll(od, 1, 0))
-        ev_after = jnp.where(last, 0.0, pltpu.roll(ev, WL - 1, 0))
-        cols_of.append((od + ev_after, ev + od, od_before + ev))
-
     for b in range(3):
         for half in range(2):
             go2[half, b * 12:(b + 1) * 12, :] = go[b * 16:b * 16 + 12, half * 128:(half + 1) * 128]
     for half in range(2):
         go2[half, 36:40, :] = jnp.zeros((4, 128), F32)
+    fc = y_hi * 2 + 1 - core
+    outk = send(None, go2.at[1 - core], gocr, c_ss.at[3], c_rs.at[3], fc, s)
+
+    wout = wo32[...].astype(BF16)
+    cols_of = []
+    for r in range(4):
+        cg = dot_tn(ims[r], wout) * gate[:, r * C:(r + 1) * C]
+        ev, od = cg[0:WL], cg[WL:2 * WL]
+        od_before = jnp.where(first, 0.0, pltpu.roll(od, 1, 0))
+        ev_after = jnp.where(last, 0.0, pltpu.roll(ev, WL - 1, 0))
+        cols_of.append((od + ev_after, ev + od, od_before + ev))
 
     def put_grad(a, b, value):
         at = (3 * a + b) * C
@@ -422,17 +446,22 @@
             g32[half, at:at + C, :] = part
             gbf[half, at:at + C, :] = part.astype(BF16)
 
-    for b in range(3):
-        u0, u1, u2, u3 = (cols_of[r][b] for r in range(4))
-        outer = jnp.concatenate([u0, u1 + u2, u3], axis=0).astype(BF16)
-        inner = jnp.concatenate([u0 + u1, u2 + u3], axis=0).astype(BF16)
-        put_grad(0, b, dot_nn(latt[:, 0:3 * WL], outer))
-        put_grad(1, b, dot_nn(latt[:, WL:3 * WL], inner))
-        put_grad(2, b, dot_nn(latt[:, WL:4 * WL], outer))
-
-    fc = y_hi * 2 + 1 - core
-    main = send(None, gbf.at[1 - core], gcr, c_ss.at[0], c_rs.at[0], fc, s)
-    outk = send(None, go2.at[1 - core], gocr, c_ss.at[1], c_rs.at[1], fc, s)
+    outer = [
+        jnp.concatenate([cols_of[0][b], cols_of[1][b] + cols_of[2][b], cols_of[3][b]], axis=0)
+        .astype(BF16) for b in range(3)
+    ]
+    inner = [
+        jnp.concatenate([cols_of[0][b] + cols_of[1][b], cols_of[2][b] + cols_of[3][b]], axis=0)
+        .astype(BF16) for b in range(3)
+    ]
+    main = []
+    for a, start, stop, terms in ((0, 0, 3, outer), (1, 1, 3, inner), (2, 1, 4, outer)):
+        for b in range(3):
+            put_grad(a, b, dot_nn(latt[:, start * WL:stop * WL], terms[b]))
+        rows = pl.ds(a * 768, 768)
+        main.append(
+            send(None, gbf.at[1 - core, rows], gcr.at[rows], c_ss.at[a], c_rs.at[a], fc, s)
+        )
     outk.wait_recv()
     gsum_z = go2[core] + gocr[...]
     goz[...] = gsum_z
@@ -441,18 +470,50 @@
         send(
             None, goz, gozr.at[z], z_ss.at[0, d], z_rs.at[0, z], f, x * 16 + zd * 2 + y_lo
         )
-    main.wait_recv()
-    for n in range(4):
-        cut = slice(n * 576, (n + 1) * 576)
-        total = g32[core, cut, :] + gcr[cut, :].astype(F32)
-        x32[n] = total
-        xbf[n] = total.astype(BF16)
-
-    for d in range(1, 4):
-        xd = (x + d) % 4
-        send(
-            None, xbf.at[xd], xr.at[x], x_ss.at[0, d], x_rs.at[0, x], f, xd * 16 + z * 2 + y_lo
-        )
+
+    mine = jnp.where(core == 0, x, y)
+
+    def quarter_device(n):
+        fd = jnp.where(core == 0, f, (n // 2) * 2 + 1)
+        sd = jnp.where(core == 0, n * 16 + z * 2 + y_lo, x * 16 + z * 2 + n % 2)
+        return fd, sd
+
+    def halves_sum(half, start, count):
+        return g32[half, start:start + count, :] + gcr[start:start + count, :].astype(F32)
+
+    for part in range(2):
+        if part == 0:
+            main[0].wait_recv()
+            main[1].wait_recv()
+        else:
+            main[2].wait_recv()
+
+        @pl.when(core == 0)
+        def along_x():
+            for n in (2 * part, 2 * part + 1):
+                total = halves_sum(0, n * 576, 576)
+                x32[n] = total
+                xbf[n] = total.astype(BF16)
+
+        @pl.when(core == 1)
+        def along_y():
+            for two in range(4):
+                units = [
+                    halves_sum(1, (2 * part + h) * 576 + (2 * two + k) * 72, 72)
+                    for k in range(2) for h in range(2)
+                ]
+                for n in range(2):
+                    total = jnp.concatenate([u[36 * n:36 * n + 36] for u in units], axis=0)
+                    x32[2 * part + n, two * 144:(two + 1) * 144, :] = total
+                    xbf[2 * part + n, two * 144:(two + 1) * 144, :] = total.astype(BF16)
+
+        for n in (2 * part, 2 * part + 1):
+            send(
+                mine != n, xbf.at[n], xr.at[mine], x_ss.at[0, n], x_rs.at[0, mine],
+                *quarter_device(n),
+            )
+
+    xr[mine] = jnp.zeros((576, 128), BF16)
     gozr[z] = gsum_z
     for d in range(1, 8):
         zd = (z + d) % 8
@@ -461,15 +522,17 @@
         ).wait_recv()
     gsum_x = jnp.sum(gozr[...], axis=0)
     gox[...] = gsum_x
-    xr[x] = jnp.zeros((576, 128), BF16)
     for d in range(1, 4):
         xd = (x + d) % 4
-        remote(
-            xbf.at[xd], xr.at[xd], x_ss.at[0, d], x_rs.at[0, xd], f, xd * 16 + z * 2 + y_lo
-        ).wait_recv()
+        send(
+            None, gox, goxr.at[x], x_ss.at[1, d], x_rs.at[1, x], f, xd * 16 + z * 2 + y_lo
+        )
+    for n in range(4):
+        copy = remote(xbf.at[n], xr.at[n], x_ss.at[0, n], x_rs.at[0, n], *quarter_device(n))
+        guard(mine != n, copy.wait_recv)
     for n in range(8):
         cut = slice(n * 72, (n + 1) * 72)
-        total = x32[x, cut, :]
+        total = x32[mine, cut, :]
         for k in range(4):
             total = total + xr[k, cut, :].astype(F32)
         z32[n] = total
@@ -479,11 +542,6 @@
         zd = (z + d) % 8
         send(
             None, zbf.at[zd], zr.at[z], z_ss.at[1, d], z_rs.at[1, z], f, x * 16 + zd * 2 + y_lo
-        )
-    for d in range(1, 4):
-        xd = (x + d) % 4
-        send(
-            None, gox, goxr.at[x], x_ss.at[1, d], x_rs.at[1, x], f, xd * 16 + z * 2 + y_lo
         )
     goxr[x] = gsum_x
     zr[z] = jnp.zeros((80, 128), BF16)
@@ -493,6 +551,11 @@
             gox, goxr.at[xd], x_ss.at[1, d], x_rs.at[1, xd], f, xd * 16 + z * 2 + y_lo
         ).wait_recv()
     gsum_y = jnp.sum(goxr[...], axis=0)
+    goy[...] = gsum_y
+    for d in range(1, 8):
+        yd = (yc + d) % 8
+        send(None, goy, goyr.at[yc], y_ss.at[0, d], y_rs.at[0, yc], *yc_device(yd))
+    goyr[yc] = gsum_y
     for d in range(1, 8):
         zd = (z + d) % 8
         remote(
@@ -505,27 +568,42 @@
     for n in range(2):
         yb[n, 0:36, :] = total[36 * n:36 * n + 36]
         yb[n, 36:40, :] = jnp.zeros((4, 128), F32)
-        yb[n, 40:80, :] = gsum_y
-    for d in range(1, 8):
-        yd = (yc + d) % 8
-        send(
-            None, yb.at[(yd // 2) % 2], yr.at[yc], y_ss.at[d], y_rs.at[yc], *yc_device(yd)
-        )
-    yr[yc] = yb[y_lo]
+    slot = jnp.where(core == 0, y, 4 + x)
+    for n in range(2):
+        sd = jnp.where(core == 0, x * 16 + z * 2 + n, (2 * y_hi + n) * 16 + z * 2 + y_lo)
+        here = sd == s
+
+        @pl.when(here)
+        def keep():
+            yr[slot] = yb[n]
+
+        for j in range(4):
+            send(
+                jnp.logical_not(here & (f == j)), yb.at[n], yr.at[slot],
+                y_ss.at[1, 4 * n + j], y_rs.at[1, slot], j, sd,
+            )
+
     for d in range(1, 8):
         yd = (yc + d) % 8
         remote(
-            yb.at[0], yr.at[yd], y_ss.at[d], y_rs.at[yd], *yc_device(yd)
+            goy, goyr.at[yd], y_ss.at[0, d], y_rs.at[0, yd], *yc_device(yd)
         ).wait_recv()
     for half in range(2):
-        total = (yr[half] + yr[2 + half]) + (yr[4 + half] + yr[6 + half])
-        cut = slice(half * 128, (half + 1) * 128)
-        gconv_ref[:, cut] = total[0:36]
+        total = (goyr[half] + goyr[2 + half]) + (goyr[4 + half] + goyr[6 + half])
         for a in range(3):
             for b in range(3):
-                at = 40 + b * 12 + (2 - a) * 4
+                at = b * 12 + (2 - a) * 4
                 t = (3 * a + b) * C + half * 128
                 gout_ref[:, t:t + 128] = total[at:at + 3]
+    for half in range(2):
+        for n in range(4):
+            fd, sd = last_source(4 * half + n)
+            copy = remote(
+                yb.at[0], yr.at[4 * half + n], y_ss.at[1, 0], y_rs.at[1, 4 * half + n], fd, sd
+            )
+            guard((fd != f) | (sd != s), copy.wait_recv)
+        total = (yr[4 * half] + yr[4 * half + 1]) + (yr[4 * half + 2] + yr[4 * half + 3])
+        gconv_ref[:, half * 128:(half + 1) * 128] = total[0:36]
 
     for cond, copy in sends:
         guard(cond, copy.wait_send)
@@ -534,7 +612,7 @@
 def per_device(latents, conv_weight, conv_bias, out_weight, row_table, patch_weight, pos_embed,
                proj_weight, text_embed):
     vmem = pl.BlockSpec(memory_space=pltpu.VMEM)
-    hbm = pl.BlockSpec(memory_space=pl.ANY)
+    hbm = pl.BlockSpec(memory_space=pltpu.HBM)
     V = pltpu.VMEM
     dma = pltpu.SemaphoreType.DMA
     reward, gconv, gout = pl.pallas_call(
@@ -544,9 +622,10 @@
             jax.ShapeDtypeStruct((36, C), F32),
             jax.ShapeDtypeStruct((3, 9 * C), F32),
         ),
-        in_specs=[hbm, hbm, vmem, vmem, vmem, hbm, hbm, hbm, vmem],
+        in_specs=[hbm] * 9,
         out_specs=(pl.BlockSpec(memory_space=pltpu.SMEM), vmem, vmem),
         scratch_shapes=[
+            V((1, C), F32), V((3, 9 * C), BF16), V((1, IMG), jnp.int32), V((1, EMB), F32),
             V((4, WL, C), BF16),
             V((3, 3 * C, C), BF16),
             V((4 * WL, 3 * C), BF16),
@@ -577,20 +656,22 @@
             V((8, 80, 128), BF16),
             V((8, 72, 128), F32),
             V((8, 80, 128), BF16),
-            V((2, 80, 128), F32),
-            V((8, 80, 128), F32),
+            V((2, 40, 128), F32),
+            V((8, 40, 128), F32),
             V((2, 40, 128), F32),
             V((40, 128), F32),
             V((40, 128), F32),
             V((8, 40, 128), F32),
             V((40, 128), F32),
             V((4, 40, 128), F32),
-            dma((14,)), dma((2,)), dma((2,)), dma((9,)), dma((9,)), dma((16,)), dma((16,)),
-            dma((2,)), dma((2,)), dma((2, 4)), dma((2, 4)), dma((2, 8)), dma((2, 8)),
-            dma((8,)), dma((8,)),
+            V((40, 128), F32),
+            V((8, 40, 128), F32),
+            dma((18,)), dma((2,)), dma((2,)), dma((9,)), dma((9,)), dma((16,)), dma((16,)),
+            dma((4,)), dma((4,)), dma((2, 4)), dma((2, 4)), dma((2, 8)), dma((2, 8)),
+            dma((2, 8)), dma((2, 8)),
         ],
         compiler_params=pltpu.CompilerParams(
-            collective_id=0, has_side_effects=True, vmem_limit_bytes=50 * 1024 * 1024
+            collective_id=0, has_side_effects=True, vmem_limit_bytes=60 * 1024 * 1024
         ),
     )(
         latents, conv_weight, conv_bias.reshape(1, C), out_weight, row_table, patch_weight,

time: 70.7 us -> 59.1 us (0.84)
  local copies, waits for them, and re-layouts: 8.64 us -> 2.79 us
  Pallas kernels: 59.3 us -> 53.6 us
    unnamed x18 -> x2, local copies, waits for them, and re-layouts: 8.64 us -> 2.79 us
    pallas_call x1, Pallas kernels: 59.3 us -> 53.6 us  [per_device(): pl.pallas_call(kernel, out_shape=(jax.ShapeDtypeStruct((1,), F32), jax.Sh...]
where the time goes in v2:
time: 59.1 us; the launch traced here: 58.9 us
  Pallas kernels  53.6 us (91%)
  local copies, waits for them, and re-layouts  2.79 us (5%)
  between operations  2.46 us (4%)
    pallas_call x1, Pallas kernels, per_device(): pl.pallas_call(kernel, out_shape=(jax.ShapeDtypeStruct((1,), F32), jax.Sh...  53.6 us
    unnamed x2, local copies, waits for them, and re-layouts  2.79 us

profile of v2, /device:TPU:1, one launch (start us, length us, event | category | flops | bytes accessed | tf_op | source)
XLA Modules:
  0.0 58.9 jit_solution(12820226056404317515)
XLA Ops:
  0.6 53.6 %shard_map.112 = (f32[1]{0:T(128)}, f32[36,256]{1,0:T(8,128)}, f32[3,2304]{1,0:T(4,128)}) custom-call(bf16[1,2,128,256]{3,2,1,0:T(8,128)(2,1)} %lat_hbm.1, bf16[2304,256]{1,0:T(8,128)(2,1)} %cw_hbm.1, f32[1,256]{1,0:T(1,128)} %bitcast.3, bf16[3,2304]{1,0:T(4,128)(2,1)} %ow_hbm.1, s32[1,224]{1,0:T(1,128)} %table_hbm.1, bf16[588,1280]{1,0:T(8,128)(2,1)} %pw_hbm.1, ...), custom_call_target="tpu_custom_call" | custom-call | tf_op jit(solution)/shard_map/pallas_call | solution.py:618
  55.0 1.4 %copy.16 = f32[36,256]{1,0:T(8,128)} copy(f32[36,256]{1,0:T(8,128)} %get-tuple-element.7) | data formatting | bytes 73728
  56.4 1.4 %copy.17 = f32[3,2304]{1,0:T(4,128)} copy(f32[3,2304]{1,0:T(4,128)} %get-tuple-element.8) | data formatting | bytes 55296

commit v3 on v2

--- a/solution.py
+++ b/solution.py
@@ -62,7 +62,7 @@
     g32, gbf, gcr, xbf, x32, xr, zbf, z32, zr, yb, yr,
     go2, gocr, goz, gozr, gox, goxr, goy, goyr,
     loc_sem, halo_ss, halo_rs, gat_ss, gat_rs, pool_ss, pool_rs,
-    c_ss, c_rs, x_ss, x_rs, z_ss, z_rs, y_ss, y_rs,
+    c_ss, c_rs, u_ss, u_rs, x_ss, x_rs, z_ss, z_rs, y_ss, y_rs, flood_sem,
 ):
     f = lax.axis_index("frame")
     s = lax.axis_index("slab")
@@ -98,11 +98,9 @@
         greet((q == 3) & (p < GROUPS - 1), f, 4 * p + 4 + v)
     greet((q < 3) & (p < GROUPS - 1), f, 4 * p + 4)
     greet((q == 3) & (p < GROUPS - 2), f, 4 * p + 8)
-    for d in range(1, GROUPS):
-        greet(None, f, 4 * ((p + d) % GROUPS) + q)
     for d in range(1, 4):
         greet(None, f, ((x + d) % 4) * 16 + z * 2 + y_lo)
-    for d in range(1, 8):
+    for d in (2, 6):
         greet(None, f, x * 16 + ((z + d) % 8) * 2 + y_lo)
     yc = y_hi * 4 + y_lo * 2 + core
 
@@ -112,16 +110,12 @@
     for d in range(1, 8):
         greet(None, *yc_device((yc + d) % 8))
     y = y_hi * 2 + y_lo
-    own_pair = x // 2 == y_hi
 
     def last_source(slot):
         if slot < 4:
             return (slot // 2) * 2, x * 16 + z * 2 + slot % 2
         return (x // 2) * 2 + 1, (slot - 4) * 16 + z * 2 + y_lo
 
-    for slot in range(4, 8):
-        greet((core == 0) | (y_hi != x // 2) | (x != slot - 4), *last_source(slot))
-
     def one(cond):
         return jnp.where(cond, 1, 0)
 
@@ -129,7 +123,7 @@
         one(s > 0) + one(s < N_SLAB - 1)
         + 3 + one(p < GROUPS - 1) + one(p > 0)
         + one((q == 0) & (p > 0)) * 3 + one((q == 0) & (p > 1))
-        + 15 + 3 + 7 + 7 + jnp.where(core == 0, 0, jnp.where(own_pair, 7, 8))
+        + 3 + 2 + 7
     )
 
     loads = []
@@ -161,6 +155,19 @@
 
     pl.semaphore_wait(barrier, expected)
 
+    def flood(stage):
+        for n, d in enumerate((2, 6)):
+            pl.semaphore_signal(
+                flood_sem.at[2 * stage + n], inc=1,
+                device_id=(f, x * 16 + ((z + d) % 8) * 2 + y_lo), device_id_type=MESH,
+            )
+
+    def flood_wait(stage):
+        for n in range(2):
+            pl.semaphore_wait(flood_sem.at[2 * stage + n], 1)
+
+    flood(0)
+
     sends = []
 
     def remote(src, dst, ssem, rsem, fd, sd):
@@ -202,37 +209,55 @@
     first = iota((WL, C), 0) == 0
     last = iota((WL, C), 0) == WL - 1
 
-    def conv_rows(rows):
-        count = len(rows)
-        for n, r6 in enumerate(rows):
-            for a in range(3):
-                lcat[n * WL:(n + 1) * WL, a * C:(a + 1) * C] = lat4[lat_row(r6, a)]
-        for b in range(3):
-            zbuf[b, 0:count * WL] = dot_nn(lcat[0:count * WL, :], wb[b])
-        for n, r6 in enumerate(rows):
-            here = slice(n * WL, (n + 1) * WL)
-            z0, z1, z2 = zbuf[0, here], zbuf[1, here], zbuf[2, here]
-            before = jnp.where(first, 0.0, pltpu.roll(z0, 1, 0))
-            after = jnp.where(last, 0.0, pltpu.roll(z2, WL - 1, 0))
-            for pc, total in ((0, before + z1 + z2), (1, z0 + z1 + after)):
-                total = total + bias
-                hidden = total / (1.0 + jnp.exp(-total))
-                if r6 == 0:
-                    hidden = jnp.where(s > 0, hidden, 0.0)
-                elif r6 == 5:
-                    hidden = jnp.where(s < N_SLAB - 1, hidden, 0.0)
-                else:
-                    gate[pc * WL:(pc + 1) * WL, (r6 - 1) * C:r6 * C] = total
-                hbuf[pc * WL:(pc + 1) * WL, r6 * C:(r6 + 1) * C] = hidden.astype(BF16)
+    def activate(r6, z0, z1, z2):
+        before = jnp.where(first, 0.0, pltpu.roll(z0, 1, 0))
+        after = jnp.where(last, 0.0, pltpu.roll(z2, WL - 1, 0))
+        for pc, total in ((0, before + z1 + z2), (1, z0 + z1 + after)):
+            total = total + bias
+            hidden = total * (0.5 + 0.5 * jnp.tanh(0.5 * total))
+            if r6 == 0:
+                hidden = jnp.where(s > 0, hidden, 0.0)
+            elif r6 == 5:
+                hidden = jnp.where(s < N_SLAB - 1, hidden, 0.0)
+            else:
+                gate[pc * WL:(pc + 1) * WL, (r6 - 1) * C:r6 * C] = total
+            hbuf[pc * WL:(pc + 1) * WL, r6 * C:(r6 + 1) * C] = hidden.astype(BF16)
 
     lat_load.wait()
     for copy in w_loads:
         copy.wait()
-    conv_rows([2, 3])
+
+    for n, r6 in enumerate((2, 3)):
+        for a in range(3):
+            lcat[n * WL:(n + 1) * WL, a * C:(a + 1) * C] = lat4[lat_row(r6, a)]
+    for b in range(3):
+        zbuf[b, 0:2 * WL] = dot_nn(lcat[0:2 * WL, :], wb[b])
+    for n, r6 in enumerate((2, 3)):
+        here = slice(n * WL, (n + 1) * WL)
+        activate(r6, zbuf[0, here], zbuf[1, here], zbuf[2, here])
+    for b in range(3):
+        top, low = lat4[1], lat4[2]
+        zbuf[b, 0:WL] = dot_nn(top, wb[b, 2 * C:3 * C])
+        zbuf[b, WL:2 * WL] = dot_nn(jnp.concatenate([top, top], axis=1), wb[b, C:3 * C])
+        zbuf[b, 2 * WL:3 * WL] = dot_nn(jnp.concatenate([low, low], axis=1), wb[b, 0:2 * C])
+        zbuf[b, 3 * WL:4 * WL] = dot_nn(low, wb[b, 0:C])
 
     guard(s < N_SLAB - 1, up.wait_recv)
     guard(s > 0, down.wait_recv)
-    conv_rows([0, 1, 4, 5])
+    flood_wait(0)
+    flood(1)
+    for near, far, edge, inner_tap, outer_tap in ((1, 0, 0, 0, 1), (4, 5, 3, 2, 1)):
+        halo_row = lat4[edge]
+        near_z, far_z = [], []
+        for b in range(3):
+            one_tap = dot_nn(halo_row, wb[b, inner_tap * C:(inner_tap + 1) * C])
+            two_taps = one_tap + dot_nn(halo_row, wb[b, outer_tap * C:(outer_tap + 1) * C])
+            n = 0 if near == 1 else 3
+            far_z.append(zbuf[b, n * WL:(n + 1) * WL] + two_taps)
+            n = 1 if near == 1 else 2
+            near_z.append(zbuf[b, n * WL:(n + 1) * WL] + one_tap)
+        activate(far, *far_z)
+        activate(near, *near_z)
 
     res = dot_nt(wd32[...].astype(BF16), hbuf[...])
     even, odd = res[:, 0:WL], res[:, WL:2 * WL]
@@ -312,6 +337,7 @@
         jnp.where(low_half, 4 * p + 4, 4 * p + 8),
     )
 
+    flood_wait(1)
     crop = dot_nn(pick, dall[...].reshape(144, 256)) * inv
     ct[...] = crop.T
     lane16 = iota((16, 128), 1) < 64
@@ -347,7 +373,7 @@
     for n in range(4):
         cut = slice(n * C, (n + 1) * C)
         total = gate[:, cut]
-        sig = 1.0 / (1.0 + jnp.exp(-total))
+        sig = 0.5 + 0.5 * jnp.tanh(0.5 * total)
         gate[:, cut] = sig * (1.0 + total * (1.0 - sig))
     for n in range(4):
         latt[:, n * WL:(n + 1) * WL] = lat4[n].astype(F32).T.astype(BF16)
@@ -422,11 +448,11 @@
         im = jnp.concatenate([igs[b, 4 * r:4 * r + 16, :] for b in range(3)], axis=0).astype(BF16)
         ims.append(im)
         go = go + dot_nn(im, hbuf[:, (r + 1) * C:(r + 2) * C])
-    for b in range(3):
-        for half in range(2):
-            go2[half, b * 12:(b + 1) * 12, :] = go[b * 16:b * 16 + 12, half * 128:(half + 1) * 128]
     for half in range(2):
-        go2[half, 36:40, :] = jnp.zeros((4, 128), F32)
+        go2[half, 27:32, :] = jnp.zeros((5, 128), F32)
+        for t in range(9):
+            at = (t % 3) * 16 + (2 - t // 3) * 4
+            go2[half, 3 * t:3 * t + 3, :] = go[at:at + 3, half * 128:(half + 1) * 128]
     fc = y_hi * 2 + 1 - core
     outk = send(None, go2.at[1 - core], gocr, c_ss.at[3], c_rs.at[3], fc, s)
 
@@ -454,6 +480,15 @@
         jnp.concatenate([cols_of[0][b] + cols_of[1][b], cols_of[2][b] + cols_of[3][b]], axis=0)
         .astype(BF16) for b in range(3)
     ]
+    outk.wait_recv()
+    gsum_z = go2[core] + gocr[...]
+    goz[...] = gsum_z
+    for d in range(1, 8):
+        zd = (z + d) % 8
+        send(
+            None, goz, gozr.at[z], z_ss.at[0, d], z_rs.at[0, z], f, x * 16 + zd * 2 + y_lo
+        )
+
     main = []
     for a, start, stop, terms in ((0, 0, 3, outer), (1, 1, 3, inner), (2, 1, 4, outer)):
         for b in range(3):
@@ -462,14 +497,6 @@
         main.append(
             send(None, gbf.at[1 - core, rows], gcr.at[rows], c_ss.at[a], c_rs.at[a], fc, s)
         )
-    outk.wait_recv()
-    gsum_z = go2[core] + gocr[...]
-    goz[...] = gsum_z
-    for d in range(1, 8):
-        zd = (z + d) % 8
-        send(
-            None, goz, gozr.at[z], z_ss.at[0, d], z_rs.at[0, z], f, x * 16 + zd * 2 + y_lo
-        )
 
     mine = jnp.where(core == 0, x, y)
 
@@ -481,39 +508,62 @@
     def halves_sum(half, start, count):
         return g32[half, start:start + count, :] + gcr[start:start + count, :].astype(F32)
 
-    for part in range(2):
-        if part == 0:
-            main[0].wait_recv()
-            main[1].wait_recv()
-        else:
-            main[2].wait_recv()
-
-        @pl.when(core == 0)
-        def along_x():
-            for n in (2 * part, 2 * part + 1):
-                total = halves_sum(0, n * 576, 576)
-                x32[n] = total
-                xbf[n] = total.astype(BF16)
-
-        @pl.when(core == 1)
-        def along_y():
-            for two in range(4):
+    for w in range(4):
+        for part in range(2):
+            if w == 0 and part == 0:
+                main[0].wait_recv()
+                main[1].wait_recv()
+            elif w == 0:
+                main[2].wait_recv()
+
+            @pl.when(core == 0)
+            def along_x():
+                for n in (2 * part, 2 * part + 1):
+                    total = jnp.concatenate(
+                        [halves_sum(0, n * 576 + zd * 72, 72) for zd in (w, w + 4)], axis=0
+                    )
+                    x32[n, w] = total
+                    xbf[n, w] = total.astype(BF16)
+
+            @pl.when(core == 1)
+            def along_y():
                 units = [
-                    halves_sum(1, (2 * part + h) * 576 + (2 * two + k) * 72, 72)
-                    for k in range(2) for h in range(2)
+                    halves_sum(1, (2 * part + h) * 576 + zd * 72, 72)
+                    for zd in (w, w + 4) for h in range(2)
                 ]
                 for n in range(2):
                     total = jnp.concatenate([u[36 * n:36 * n + 36] for u in units], axis=0)
-                    x32[2 * part + n, two * 144:(two + 1) * 144, :] = total
-                    xbf[2 * part + n, two * 144:(two + 1) * 144, :] = total.astype(BF16)
-
-        for n in (2 * part, 2 * part + 1):
+                    x32[2 * part + n, w] = total
+                    xbf[2 * part + n, w] = total.astype(BF16)
+
+            for n in (2 * part, 2 * part + 1):
+                send(
+                    mine != n, xbf.at[n, w], xr.at[w, mine], u_ss.at[w, n], u_rs.at[w, mine],
+                    *quarter_device(n),
+                )
+
+    for w in range(4):
+        xr[w, mine] = jnp.zeros((144, 128), BF16)
+    zr[z] = jnp.zeros((80, 128), BF16)
+    for w in range(4):
+        for n in range(4):
+            copy = remote(
+                xbf.at[n, w], xr.at[w, n], u_ss.at[w, n], u_rs.at[w, n], *quarter_device(n)
+            )
+            guard(mine != n, copy.wait_recv)
+        for k in range(2):
+            zd = w + 4 * k
+            cut = slice(k * 72, (k + 1) * 72)
+            total = x32[mine, w, cut, :]
+            for n in range(4):
+                total = total + xr[w, n, cut, :].astype(F32)
+            z32[zd] = total
+            zbf[zd] = jnp.concatenate([total, jnp.zeros((8, 128), F32)], axis=0).astype(BF16)
             send(
-                mine != n, xbf.at[n], xr.at[mine], x_ss.at[0, n], x_rs.at[0, mine],
-                *quarter_device(n),
+                z != zd, zbf.at[zd], zr.at[z], z_ss.at[1, zd], z_rs.at[1, z],
+                f, x * 16 + zd * 2 + y_lo,
             )
 
-    xr[mine] = jnp.zeros((576, 128), BF16)
     gozr[z] = gsum_z
     for d in range(1, 8):
         zd = (z + d) % 8
@@ -524,31 +574,12 @@
     gox[...] = gsum_x
     for d in range(1, 4):
         xd = (x + d) % 4
-        send(
-            None, gox, goxr.at[x], x_ss.at[1, d], x_rs.at[1, x], f, xd * 16 + z * 2 + y_lo
-        )
-    for n in range(4):
-        copy = remote(xbf.at[n], xr.at[n], x_ss.at[0, n], x_rs.at[0, n], *quarter_device(n))
-        guard(mine != n, copy.wait_recv)
-    for n in range(8):
-        cut = slice(n * 72, (n + 1) * 72)
-        total = x32[mine, cut, :]
-        for k in range(4):
-            total = total + xr[k, cut, :].astype(F32)
-        z32[n] = total
-        zbf[n] = jnp.concatenate([total, jnp.zeros((8, 128), F32)], axis=0).astype(BF16)
-
-    for d in range(1, 8):
-        zd = (z + d) % 8
-        send(
-            None, zbf.at[zd], zr.at[z], z_ss.at[1, d], z_rs.at[1, z], f, x * 16 + zd * 2 + y_lo
-        )
+        send(None, gox, goxr.at[x], x_ss.at[d], x_rs.at[x], f, xd * 16 + z * 2 + y_lo)
     goxr[x] = gsum_x
-    zr[z] = jnp.zeros((80, 128), BF16)
     for d in range(1, 4):
         xd = (x + d) % 4
         remote(
-            gox, goxr.at[xd], x_ss.at[1, d], x_rs.at[1, xd], f, xd * 16 + z * 2 + y_lo
+            gox, goxr.at[xd], x_ss.at[d], x_rs.at[xd], f, xd * 16 + z * 2 + y_lo
         ).wait_recv()
     gsum_y = jnp.sum(goxr[...], axis=0)
     goy[...] = gsum_y
@@ -556,6 +587,7 @@
         yd = (yc + d) % 8
         send(None, goy, goyr.at[yc], y_ss.at[0, d], y_rs.at[0, yc], *yc_device(yd))
     goyr[yc] = gsum_y
+
     for d in range(1, 8):
         zd = (z + d) % 8
         remote(
@@ -590,11 +622,8 @@
         ).wait_recv()
     for half in range(2):
         total = (goyr[half] + goyr[2 + half]) + (goyr[4 + half] + goyr[6 + half])
-        for a in range(3):
-            for b in range(3):
-                at = b * 12 + (2 - a) * 4
-                t = (3 * a + b) * C + half * 128
-                gout_ref[:, t:t + 128] = total[at:at + 3]
+        for t in range(9):
+            gout_ref[:, t * C + half * 128:t * C + (half + 1) * 128] = total[3 * t:3 * t + 3]
     for half in range(2):
         for n in range(4):
             fd, sd = last_source(4 * half + n)
@@ -628,7 +657,7 @@
             V((1, C), F32), V((3, 9 * C), BF16), V((1, IMG), jnp.int32), V((1, EMB), F32),
             V((4, WL, C), BF16),
             V((3, 3 * C, C), BF16),
-            V((4 * WL, 3 * C), BF16),
+            V((2 * WL, 3 * C), BF16),
             V((3, 4 * WL, C), F32),
             V((2 * WL, 6 * C), BF16),
             V((2 * WL, 4 * C), F32),
@@ -650,25 +679,26 @@
             V((2, 9 * C, 128), F32),
             V((2, 9 * C, 128), BF16),
             V((9 * C, 128), BF16),
-            V((4, 576, 128), BF16),
-            V((4, 576, 128), F32),
-            V((4, 576, 128), BF16),
+            V((4, 4, 144, 128), BF16),
+            V((4, 4, 144, 128), F32),
+            V((4, 4, 144, 128), BF16),
             V((8, 80, 128), BF16),
             V((8, 72, 128), F32),
             V((8, 80, 128), BF16),
             V((2, 40, 128), F32),
             V((8, 40, 128), F32),
-            V((2, 40, 128), F32),
-            V((40, 128), F32),
-            V((40, 128), F32),
-            V((8, 40, 128), F32),
-            V((40, 128), F32),
-            V((4, 40, 128), F32),
-            V((40, 128), F32),
-            V((8, 40, 128), F32),
+            V((2, 32, 128), F32),
+            V((32, 128), F32),
+            V((32, 128), F32),
+            V((8, 32, 128), F32),
+            V((32, 128), F32),
+            V((4, 32, 128), F32),
+            V((32, 128), F32),
+            V((8, 32, 128), F32),
             dma((18,)), dma((2,)), dma((2,)), dma((9,)), dma((9,)), dma((16,)), dma((16,)),
-            dma((4,)), dma((4,)), dma((2, 4)), dma((2, 4)), dma((2, 8)), dma((2, 8)),
+            dma((4,)), dma((4,)), dma((4, 4)), dma((4, 4)), dma((4,)), dma((4,)),
             dma((2, 8)), dma((2, 8)),
+            dma((2, 8)), dma((2, 8)), pltpu.SemaphoreType.REGULAR((4,)),
         ],
         compiler_params=pltpu.CompilerParams(
             collective_id=0, has_side_effects=True, vmem_limit_bytes=60 * 1024 * 1024

time: 59.1 us -> 56.8 us (0.961)
  Pallas kernels: 53.6 us -> 51.3 us
    pallas_call x1, Pallas kernels: 53.6 us -> 51.3 us  [per_device(): pl.pallas_call(kernel, out_shape=(jax.ShapeDtypeStruct((1,), F32), jax.Sh...]
where the time goes in v3:
time: 56.8 us; the launch traced here: 56.6 us
  Pallas kernels  51.3 us (90%)
  local copies, waits for them, and re-layouts  2.79 us (5%)
  between operations  2.46 us (4%)
    pallas_call x1, Pallas kernels, per_device(): pl.pallas_call(kernel, out_shape=(jax.ShapeDtypeStruct((1,), F32), jax.Sh...  51.3 us
    unnamed x2, local copies, waits for them, and re-layouts  2.79 us

profile of v3, /device:TPU:1, one launch (start us, length us, event | category | flops | bytes accessed | tf_op | source)
XLA Modules:
  0.0 56.6 jit_solution(10479828945707999516)
XLA Ops:
  0.6 51.3 %shard_map.112 = (f32[1]{0:T(128)}, f32[36,256]{1,0:T(8,128)}, f32[3,2304]{1,0:T(4,128)}) custom-call(bf16[1,2,128,256]{3,2,1,0:T(8,128)(2,1)} %lat_hbm.1, bf16[2304,256]{1,0:T(8,128)(2,1)} %cw_hbm.1, f32[1,256]{1,0:T(1,128)} %bitcast.3, bf16[3,2304]{1,0:T(4,128)(2,1)} %ow_hbm.1, s32[1,224]{1,0:T(1,128)} %table_hbm.1, bf16[588,1280]{1,0:T(8,128)(2,1)} %pw_hbm.1, ...), custom_call_target="tpu_custom_call" | custom-call | tf_op jit(solution)/shard_map/pallas_call | solution.py:647
  52.7 1.4 %copy.16 = f32[36,256]{1,0:T(8,128)} copy(f32[36,256]{1,0:T(8,128)} %get-tuple-element.7) | data formatting | bytes 73728
  54.1 1.4 %copy.17 = f32[3,2304]{1,0:T(4,128)} copy(f32[3,2304]{1,0:T(4,128)} %get-tuple-element.8) | data formatting | bytes 55296

commit v4 on v3

--- a/solution.py
+++ b/solution.py
@@ -97,7 +97,6 @@
         greet((q == 0) & (p > 0), f, 4 * p - 4 + v)
         greet((q == 3) & (p < GROUPS - 1), f, 4 * p + 4 + v)
     greet((q < 3) & (p < GROUPS - 1), f, 4 * p + 4)
-    greet((q == 3) & (p < GROUPS - 2), f, 4 * p + 8)
     for d in range(1, 4):
         greet(None, f, ((x + d) % 4) * 16 + z * 2 + y_lo)
     for d in (2, 6):
@@ -122,7 +121,7 @@
     expected = (
         one(s > 0) + one(s < N_SLAB - 1)
         + 3 + one(p < GROUPS - 1) + one(p > 0)
-        + one((q == 0) & (p > 0)) * 3 + one((q == 0) & (p > 1))
+        + one((q == 0) & (p > 0)) * 3
         + 3 + 2 + 7
     )
 
@@ -168,6 +167,12 @@
 
     flood(0)
 
+    @pl.when((q == 0) & (p < GROUPS - 1))
+    def tell():
+        pl.semaphore_signal(
+            flood_sem.at[4], inc=1, device_id=(f, s + 4), device_id_type=MESH
+        )
+
     sends = []
 
     def remote(src, dst, ssem, rsem, fd, sd):
@@ -268,6 +273,10 @@
     decoded = jnp.concatenate([dec_even, dec_odd], axis=1).astype(BF16)
     dec[...] = decoded
     dall[jnp.where(low_half, q + 4, q)] = decoded
+
+    @pl.when((q == 0) & (p > 0))
+    def told():
+        pl.semaphore_wait(flood_sem.at[4], 1)
 
     def gather_send(n, cond, target, slot):
         send(cond, dec, dall.at[slot], gat_ss.at[n], gat_rs.at[slot], f, target)
@@ -341,26 +350,30 @@
     crop = dot_nn(pick, dall[...].reshape(144, 256)) * inv
     ct[...] = crop.T
     lane16 = iota((16, 128), 1) < 64
-    parts0, parts1 = [], []
+    pairs = []
     for n in range(7):
         pair = []
         for c14 in (2 * n, 2 * n + 1):
             pc, pj = patch_column(c14)
             pair.append(ct[pl.ds(pc * WL + pj, 16, stride=8), :])
-        parts0.append(jnp.where(lane16, pair[0], pltpu.roll(pair[1], 64, 1)))
-        parts1.append(jnp.where(lane16, pltpu.roll(pair[0], 64, 1), pair[1]))
-    patches = jnp.concatenate(
-        [jnp.concatenate(parts0, axis=1), jnp.concatenate(parts1, axis=1)], axis=0
-    )
+        pairs.append(pair)
     for copy in pos_loads:
         copy.wait()
-    emb = dot_nn(jnp.concatenate(split2(patches), axis=0), pwp[...])
-    emb = emb[0:32] + emb[32:64] + pos[...].astype(F32)
-    centred = emb - jnp.mean(emb, axis=1, keepdims=True)
-    sigma = jnp.sqrt(jnp.mean(centred * centred, axis=1, keepdims=True) + EPS)
-    normed = centred / sigma
-    ybuf[...] = normed
-    gsum = jnp.sum(normed[0:16], axis=0, keepdims=True)
+
+    def embed(parts, rows):
+        patches = jnp.concatenate(parts, axis=1)
+        emb = dot_nn(jnp.concatenate(split2(patches), axis=0), pwp[...])
+        emb = emb[0:16] + emb[16:32] + pos[rows, :].astype(F32)
+        centred = emb - jnp.mean(emb, axis=1, keepdims=True)
+        sigma = jnp.sqrt(jnp.mean(centred * centred, axis=1, keepdims=True) + EPS)
+        normed = centred / sigma
+        ybuf[rows, :] = normed
+        return normed, sigma
+
+    normed, sigma0 = embed(
+        [jnp.where(lane16, one_, pltpu.roll(two, 64, 1)) for one_, two in pairs], slice(0, 16)
+    )
+    gsum = jnp.sum(normed, axis=0, keepdims=True)
     psend[...] = gsum
     precv[p] = gsum
 
@@ -369,6 +382,11 @@
             None, psend, precv.at[p], pool_ss.at[d], pool_rs.at[p],
             f, 4 * ((p + d) % GROUPS) + q,
         )
+
+    sigma1 = embed(
+        [jnp.where(lane16, pltpu.roll(one_, 64, 1), two) for one_, two in pairs], slice(16, 32)
+    )[1]
+    sigma = jnp.concatenate([sigma0, sigma1], axis=0)
 
     for n in range(4):
         cut = slice(n * C, (n + 1) * C)
@@ -482,7 +500,7 @@
     ]
     outk.wait_recv()
     gsum_z = go2[core] + gocr[...]
-    goz[...] = gsum_z
+    goz[...] = gsum_z.astype(BF16)
     for d in range(1, 8):
         zd = (z + d) % 8
         send(
@@ -563,18 +581,19 @@
                 z != zd, zbf.at[zd], zr.at[z], z_ss.at[1, zd], z_rs.at[1, z],
                 f, x * 16 + zd * 2 + y_lo,
             )
-
-    gozr[z] = gsum_z
-    for d in range(1, 8):
-        zd = (z + d) % 8
-        remote(
-            goz, gozr.at[zd], z_ss.at[0, d], z_rs.at[0, zd], f, x * 16 + zd * 2 + y_lo
-        ).wait_recv()
-    gsum_x = jnp.sum(gozr[...], axis=0)
-    gox[...] = gsum_x
-    for d in range(1, 4):
-        xd = (x + d) % 4
-        send(None, gox, goxr.at[x], x_ss.at[d], x_rs.at[x], f, xd * 16 + z * 2 + y_lo)
+        if w == 1:
+            gozr[z] = jnp.zeros((32, 128), BF16)
+            for d in range(1, 8):
+                zd = (z + d) % 8
+                remote(
+                    goz, gozr.at[zd], z_ss.at[0, d], z_rs.at[0, zd], f, x * 16 + zd * 2 + y_lo
+                ).wait_recv()
+            gsum_x = gsum_z + jnp.sum(gozr[...].astype(F32), axis=0)
+            gox[...] = gsum_x
+            for d in range(1, 4):
+                xd = (x + d) % 4
+                send(None, gox, goxr.at[x], x_ss.at[d], x_rs.at[x], f, xd * 16 + z * 2 + y_lo)
+
     goxr[x] = gsum_x
     for d in range(1, 4):
         xd = (x + d) % 4
@@ -689,8 +708,8 @@
             V((8, 40, 128), F32),
             V((2, 32, 128), F32),
             V((32, 128), F32),
-            V((32, 128), F32),
-            V((8, 32, 128), F32),
+            V((32, 128), BF16),
+            V((8, 32, 128), BF16),
             V((32, 128), F32),
             V((4, 32, 128), F32),
             V((32, 128), F32),
@@ -698,7 +717,7 @@
             dma((18,)), dma((2,)), dma((2,)), dma((9,)), dma((9,)), dma((16,)), dma((16,)),
             dma((4,)), dma((4,)), dma((4, 4)), dma((4, 4)), dma((4,)), dma((4,)),
             dma((2, 8)), dma((2, 8)),
-            dma((2, 8)), dma((2, 8)), pltpu.SemaphoreType.REGULAR((4,)),
+            dma((2, 8)), dma((2, 8)), pltpu.SemaphoreType.REGULAR((5,)),
         ],
         compiler_params=pltpu.CompilerParams(
             collective_id=0, has_side_effects=True, vmem_limit_bytes=60 * 1024 * 1024

time: 56.8 us -> 55.2 us (0.972)
  Pallas kernels: 51.3 us -> 49.7 us
    pallas_call x1, Pallas kernels: 51.3 us -> 49.7 us  [per_device(): pl.pallas_call(kernel, out_shape=(jax.ShapeDtypeStruct((1,), F32), jax.Sh...]
where the time goes in v4:
time: 55.2 us; the launch traced here: 55 us
  Pallas kernels  49.7 us (90%)
  local copies, waits for them, and re-layouts  2.79 us (5%)
  between operations  2.46 us (4%)
    pallas_call x1, Pallas kernels, per_device(): pl.pallas_call(kernel, out_shape=(jax.ShapeDtypeStruct((1,), F32), jax.Sh...  49.7 us
    unnamed x2, local copies, waits for them, and re-layouts  2.79 us

profile of v4, /device:TPU:1, one launch (start us, length us, event | category | flops | bytes accessed | tf_op | source)
XLA Modules:
  0.0 55.0 jit_solution(7467663284201606067)
XLA Ops:
  0.6 49.7 %shard_map.112 = (f32[1]{0:T(128)}, f32[36,256]{1,0:T(8,128)}, f32[3,2304]{1,0:T(4,128)}) custom-call(bf16[1,2,128,256]{3,2,1,0:T(8,128)(2,1)} %lat_hbm.1, bf16[2304,256]{1,0:T(8,128)(2,1)} %cw_hbm.1, f32[1,256]{1,0:T(1,128)} %bitcast.3, bf16[3,2304]{1,0:T(4,128)(2,1)} %ow_hbm.1, s32[1,224]{1,0:T(1,128)} %table_hbm.1, bf16[588,1280]{1,0:T(8,128)(2,1)} %pw_hbm.1, ...), custom_call_target="tpu_custom_call" | custom-call | tf_op jit(solution)/shard_map/pallas_call | solution.py:666
  51.0 1.4 %copy.16 = f32[36,256]{1,0:T(8,128)} copy(f32[36,256]{1,0:T(8,128)} %get-tuple-element.7) | data formatting | bytes 73728
  52.4 1.4 %copy.17 = f32[3,2304]{1,0:T(4,128)} copy(f32[3,2304]{1,0:T(4,128)} %get-tuple-element.8) | data formatting | bytes 55296

commit v5 on v4

--- a/solution.py
+++ b/solution.py
@@ -57,7 +57,7 @@
     lat_hbm, cw_hbm, bias_hbm, ow_hbm, table_hbm, pw_hbm, pos_hbm, proj_hbm, text_hbm,
     reward_ref, gconv_ref, gout_ref,
     bias_ref, ow_ref, table_ref, text_ref,
-    lat4, wb, lcat, zbuf, hbuf, gate, wd32, wo32, pw, pwp, pos, proj,
+    lat4, wl, taps, hbuf, gate, wd32, wo32, pw, pwp, pos, proj,
     dec, dall, ct, gt, ybuf, psend, precv, igs, latt,
     g32, gbf, gcr, xbf, x32, xr, zbf, z32, zr, yb, yr,
     go2, gocr, goz, gozr, gox, goxr, goy, goyr,
@@ -110,11 +110,6 @@
         greet(None, *yc_device((yc + d) % 8))
     y = y_hi * 2 + y_lo
 
-    def last_source(slot):
-        if slot < 4:
-            return (slot // 2) * 2, x * 16 + z * 2 + slot % 2
-        return (x // 2) * 2 + 1, (slot - 4) * 16 + z * 2 + y_lo
-
     def one(cond):
         return jnp.where(cond, 1, 0)
 
@@ -133,24 +128,22 @@
         loads.append(copy)
         return copy
 
+    def load_parts(pairs, whole):
+        sem = loc_sem.at[len(loads)]
+        for src, dst in pairs:
+            pltpu.make_async_copy(src, dst, sem).start()
+        copy = pltpu.make_async_copy(whole, whole, sem)
+        loads.append(copy)
+        return copy
+
     lat_load = load(lat_hbm.at[0], lat4.at[pl.ds(1, 2)])
-    ow_load = load(ow_hbm, ow_ref)
-    bias_load = load(bias_hbm, bias_ref)
-    table_load = load(table_hbm, table_ref)
-    text_load = load(text_hbm, text_ref)
-    w_loads = []
-    for a in range(3):
-        for b in range(3):
-            t = 3 * a + b
-            w_loads.append(
-                load(cw_hbm.at[pl.ds(t * C, C)], wb.at[b, pl.ds(a * C, C)])
-            )
-    pw_load = load(pw_hbm, pw)
-    pos_loads = [
-        load(pos_hbm.at[pl.ds(pl.multiple_of(16 * p, 16), 16)], pos.at[pl.ds(0, 16)]),
-        load(pos_hbm.at[pl.ds(pl.multiple_of(16 * p2c, 16), 16)], pos.at[pl.ds(16, 16)]),
-    ]
-    proj_load = load(proj_hbm, proj)
+    w_load = load_parts(
+        [
+            (cw_hbm.at[pl.ds(t * C, C)], wl.at[:, pl.ds(t * C, C)])
+            for t in range(9)
+        ],
+        wl,
+    )
 
     pl.semaphore_wait(barrier, expected)
 
@@ -193,10 +186,32 @@
         sends.append((cond, copy))
         return copy
 
+    def send_part(cond, *what):
+        guard(cond, remote(*what).start)
+
+    def all_of(whole, ssem, rsem, cond=None):
+        copy = remote(whole, whole, ssem, rsem, y_hi * 2 + 1 - core, s)
+        sends.append((cond, copy))
+        guard(cond, copy.wait_recv)
+
     up = send(s > 0, lat_hbm.at[0, 0], lat4.at[3], halo_ss.at[0], halo_rs.at[1], f, s - 1)
     down = send(
         s < N_SLAB - 1, lat_hbm.at[0, 1], lat4.at[0], halo_ss.at[1], halo_rs.at[0], f, s + 1
     )
+
+    ow_load = load(ow_hbm, ow_ref)
+    bias_load = load(bias_hbm, bias_ref)
+    table_load = load(table_hbm, table_ref)
+    text_load = load(text_hbm, text_ref)
+    pw_load = load(pw_hbm, pw)
+    pos_load = load_parts(
+        [
+            (pos_hbm.at[pl.ds(pl.multiple_of(16 * p, 16), 16)], pos.at[pl.ds(0, 16)]),
+            (pos_hbm.at[pl.ds(pl.multiple_of(16 * p2c, 16), 16)], pos.at[pl.ds(16, 16)]),
+        ],
+        pos,
+    )
+    proj_load = load(proj_hbm, proj)
 
     wd32[...] = jnp.zeros_like(wd32)
     wo32[...] = jnp.zeros_like(wo32)
@@ -229,40 +244,31 @@
             hbuf[pc * WL:(pc + 1) * WL, r6 * C:(r6 + 1) * C] = hidden.astype(BF16)
 
     lat_load.wait()
-    for copy in w_loads:
-        copy.wait()
-
-    for n, r6 in enumerate((2, 3)):
-        for a in range(3):
-            lcat[n * WL:(n + 1) * WL, a * C:(a + 1) * C] = lat4[lat_row(r6, a)]
-    for b in range(3):
-        zbuf[b, 0:2 * WL] = dot_nn(lcat[0:2 * WL, :], wb[b])
-    for n, r6 in enumerate((2, 3)):
-        here = slice(n * WL, (n + 1) * WL)
-        activate(r6, zbuf[0, here], zbuf[1, here], zbuf[2, here])
-    for b in range(3):
-        top, low = lat4[1], lat4[2]
-        zbuf[b, 0:WL] = dot_nn(top, wb[b, 2 * C:3 * C])
-        zbuf[b, WL:2 * WL] = dot_nn(jnp.concatenate([top, top], axis=1), wb[b, C:3 * C])
-        zbuf[b, 2 * WL:3 * WL] = dot_nn(jnp.concatenate([low, low], axis=1), wb[b, 0:2 * C])
-        zbuf[b, 3 * WL:4 * WL] = dot_nn(low, wb[b, 0:C])
+    w_load.wait()
+
+    taps[...] = dot_nn(lat4[1:3].reshape(2 * WL, C), wl[...])
+
+    def part(row, a, b):
+        t = 3 * a + b
+        return taps[(row - 1) * WL:row * WL, t * C:(t + 1) * C]
+
+    def own_terms(r6, b):
+        rows = [(lat_row(r6, a), a) for a in range(3)]
+        return sum(part(row, a, b) for row, a in rows if row in (1, 2))
+
+    for r6 in (2, 3):
+        activate(r6, *[own_terms(r6, b) for b in range(3)])
 
     guard(s < N_SLAB - 1, up.wait_recv)
     guard(s > 0, down.wait_recv)
     flood_wait(0)
     flood(1)
-    for near, far, edge, inner_tap, outer_tap in ((1, 0, 0, 0, 1), (4, 5, 3, 2, 1)):
-        halo_row = lat4[edge]
-        near_z, far_z = [], []
-        for b in range(3):
-            one_tap = dot_nn(halo_row, wb[b, inner_tap * C:(inner_tap + 1) * C])
-            two_taps = one_tap + dot_nn(halo_row, wb[b, outer_tap * C:(outer_tap + 1) * C])
-            n = 0 if near == 1 else 3
-            far_z.append(zbuf[b, n * WL:(n + 1) * WL] + two_taps)
-            n = 1 if near == 1 else 2
-            near_z.append(zbuf[b, n * WL:(n + 1) * WL] + one_tap)
-        activate(far, *far_z)
-        activate(near, *near_z)
+    for near, far, edge, start in ((1, 0, 0, 0), (4, 5, 3, 3)):
+        halo_z = dot_nn(lat4[edge], wl[:, start * C:(start + 6) * C])
+        inner = [halo_z[:, (b if near == 1 else b + 3) * C:][:, 0:C] for b in range(3)]
+        outer = [halo_z[:, (b + 3 if near == 1 else b) * C:][:, 0:C] for b in range(3)]
+        activate(near, *[own_terms(near, b) + inner[b] for b in range(3)])
+        activate(far, *[own_terms(far, b) + (inner[b] + outer[b]) for b in range(3)])
 
     res = dot_nt(wd32[...].astype(BF16), hbuf[...])
     even, odd = res[:, 0:WL], res[:, WL:2 * WL]
@@ -357,8 +363,7 @@
             pc, pj = patch_column(c14)
             pair.append(ct[pl.ds(pc * WL + pj, 16, stride=8), :])
         pairs.append(pair)
-    for copy in pos_loads:
-        copy.wait()
+    pos_load.wait()
 
     def embed(parts, rows):
         patches = jnp.concatenate(parts, axis=1)
@@ -378,9 +383,8 @@
     precv[p] = gsum
 
     for d in range(1, GROUPS):
-        send(
-            None, psend, precv.at[p], pool_ss.at[d], pool_rs.at[p],
-            f, 4 * ((p + d) % GROUPS) + q,
+        send_part(
+            None, psend, precv.at[p], pool_ss.at[0], pool_rs.at[0], f, 4 * ((p + d) % GROUPS) + q
         )
 
     sigma1 = embed(
@@ -400,11 +404,7 @@
     text2 = jnp.sum(text * text, axis=1, keepdims=True) + 1e-06
     gt[...] = jnp.zeros_like(gt)
 
-    for d in range(1, GROUPS):
-        pd = (p + d) % GROUPS
-        remote(
-            psend, precv.at[pd], pool_ss.at[d], pool_rs.at[pd], f, 4 * pd + q
-        ).wait_recv()
+    all_of(precv.at[pl.ds(0, GROUPS - 1)], pool_ss.at[0], pool_rs.at[0])
     pooled = precv[0]
     for n in range(1, GROUPS):
         pooled = pooled + precv[n]
@@ -425,7 +425,7 @@
     norm2 = jnp.sum(projected * projected, axis=1, keepdims=True) + 1e-06
     scale = 1.0 / jnp.sqrt(norm2 * text2)
     reward = numer * scale
-    reward_ref[0] = reward[0, 0]
+    reward_ref[...] = reward
     dproj = -LOSS_SCALE * (text * scale - projected * (reward / norm2))
     dunit = jnp.sum(dot_nt(two_rows(dproj), proj[...]), axis=0, keepdims=True)
 
@@ -503,9 +503,7 @@
     goz[...] = gsum_z.astype(BF16)
     for d in range(1, 8):
         zd = (z + d) % 8
-        send(
-            None, goz, gozr.at[z], z_ss.at[0, d], z_rs.at[0, z], f, x * 16 + zd * 2 + y_lo
-        )
+        send_part(None, goz, gozr.at[z], z_ss.at[0], z_rs.at[0], f, x * 16 + zd * 2 + y_lo)
 
     main = []
     for a, start, stop, terms in ((0, 0, 3, outer), (1, 1, 3, inner), (2, 1, 4, outer)):
@@ -555,8 +553,8 @@
                     xbf[2 * part + n, w] = total.astype(BF16)
 
             for n in (2 * part, 2 * part + 1):
-                send(
-                    mine != n, xbf.at[n, w], xr.at[w, mine], u_ss.at[w, n], u_rs.at[w, mine],
+                send_part(
+                    mine != n, xbf.at[n, w], xr.at[w, mine], u_ss.at[w], u_rs.at[w],
                     *quarter_device(n),
                 )
 
@@ -564,11 +562,7 @@
         xr[w, mine] = jnp.zeros((144, 128), BF16)
     zr[z] = jnp.zeros((80, 128), BF16)
     for w in range(4):
-        for n in range(4):
-            copy = remote(
-                xbf.at[n, w], xr.at[w, n], u_ss.at[w, n], u_rs.at[w, n], *quarter_device(n)
-            )
-            guard(mine != n, copy.wait_recv)
+        all_of(xr.at[w, pl.ds(0, 3)], u_ss.at[w], u_rs.at[w])
         for k in range(2):
             zd = w + 4 * k
             cut = slice(k * 72, (k + 1) * 72)
@@ -577,41 +571,30 @@
                 total = total + xr[w, n, cut, :].astype(F32)
             z32[zd] = total
             zbf[zd] = jnp.concatenate([total, jnp.zeros((8, 128), F32)], axis=0).astype(BF16)
-            send(
-                z != zd, zbf.at[zd], zr.at[z], z_ss.at[1, zd], z_rs.at[1, z],
-                f, x * 16 + zd * 2 + y_lo,
+            send_part(
+                z != zd, zbf.at[zd], zr.at[z], z_ss.at[1], z_rs.at[1], f, x * 16 + zd * 2 + y_lo
             )
         if w == 1:
             gozr[z] = jnp.zeros((32, 128), BF16)
-            for d in range(1, 8):
-                zd = (z + d) % 8
-                remote(
-                    goz, gozr.at[zd], z_ss.at[0, d], z_rs.at[0, zd], f, x * 16 + zd * 2 + y_lo
-                ).wait_recv()
+            all_of(gozr.at[pl.ds(0, 7)], z_ss.at[0], z_rs.at[0])
             gsum_x = gsum_z + jnp.sum(gozr[...].astype(F32), axis=0)
             gox[...] = gsum_x
             for d in range(1, 4):
                 xd = (x + d) % 4
-                send(None, gox, goxr.at[x], x_ss.at[d], x_rs.at[x], f, xd * 16 + z * 2 + y_lo)
+                send_part(
+                    None, gox, goxr.at[x], x_ss.at[0], x_rs.at[0], f, xd * 16 + z * 2 + y_lo
+                )
 
     goxr[x] = gsum_x
-    for d in range(1, 4):
-        xd = (x + d) % 4
-        remote(
-            gox, goxr.at[xd], x_ss.at[d], x_rs.at[xd], f, xd * 16 + z * 2 + y_lo
-        ).wait_recv()
+    all_of(goxr.at[pl.ds(0, 3)], x_ss.at[0], x_rs.at[0])
     gsum_y = jnp.sum(goxr[...], axis=0)
     goy[...] = gsum_y
     for d in range(1, 8):
         yd = (yc + d) % 8
-        send(None, goy, goyr.at[yc], y_ss.at[0, d], y_rs.at[0, yc], *yc_device(yd))
+        send_part(None, goy, goyr.at[yc], y_ss.at[0], y_rs.at[0], *yc_device(yd))
     goyr[yc] = gsum_y
 
-    for d in range(1, 8):
-        zd = (z + d) % 8
-        remote(
-            zbf.at[zd], zr.at[zd], z_ss.at[1, d], z_rs.at[1, zd], f, x * 16 + zd * 2 + y_lo
-        ).wait_recv()
+    all_of(zr.at[pl.ds(0, 7)], z_ss.at[1], z_rs.at[1])
     total = z32[z]
     for n in range(8):
         total = total + zr[n, 0:72, :].astype(F32)
@@ -629,27 +612,20 @@
             yr[slot] = yb[n]
 
         for j in range(4):
-            send(
+            send_part(
                 jnp.logical_not(here & (f == j)), yb.at[n], yr.at[slot],
-                y_ss.at[1, 4 * n + j], y_rs.at[1, slot], j, sd,
+                y_ss.at[1], y_rs.at[1], j, sd,
             )
 
-    for d in range(1, 8):
-        yd = (yc + d) % 8
-        remote(
-            goy, goyr.at[yd], y_ss.at[0, d], y_rs.at[0, yd], *yc_device(yd)
-        ).wait_recv()
+    all_of(goyr.at[pl.ds(0, 7)], y_ss.at[0], y_rs.at[0])
     for half in range(2):
         total = (goyr[half] + goyr[2 + half]) + (goyr[4 + half] + goyr[6 + half])
         for t in range(9):
             gout_ref[:, t * C + half * 128:t * C + (half + 1) * 128] = total[3 * t:3 * t + 3]
+    seven = (core == 0) | (x // 2 == y_hi)
+    all_of(yr.at[pl.ds(0, 7)], y_ss.at[1], y_rs.at[1], seven)
+    all_of(yr, y_ss.at[1], y_rs.at[1], jnp.logical_not(seven))
     for half in range(2):
-        for n in range(4):
-            fd, sd = last_source(4 * half + n)
-            copy = remote(
-                yb.at[0], yr.at[4 * half + n], y_ss.at[1, 0], y_rs.at[1, 4 * half + n], fd, sd
-            )
-            guard((fd != f) | (sd != s), copy.wait_recv)
         total = (yr[4 * half] + yr[4 * half + 1]) + (yr[4 * half + 2] + yr[4 * half + 3])
         gconv_ref[:, half * 128:(half + 1) * 128] = total[0:36]
 
@@ -666,18 +642,17 @@
     reward, gconv, gout = pl.pallas_call(
         kernel,
         out_shape=(
-            jax.ShapeDtypeStruct((1,), F32),
+            jax.ShapeDtypeStruct((1, 1), F32),
             jax.ShapeDtypeStruct((36, C), F32),
             jax.ShapeDtypeStruct((3, 9 * C), F32),
         ),
         in_specs=[hbm] * 9,
-        out_specs=(pl.BlockSpec(memory_space=pltpu.SMEM), vmem, vmem),
+        out_specs=(vmem, vmem, vmem),
         scratch_shapes=[
             V((1, C), F32), V((3, 9 * C), BF16), V((1, IMG), jnp.int32), V((1, EMB), F32),
             V((4, WL, C), BF16),
-            V((3, 3 * C, C), BF16),
-            V((2 * WL, 3 * C), BF16),
-            V((3, 4 * WL, C), F32),
+            V((C, 9 * C), BF16),
+            V((2 * WL, 9 * C), F32),
             V((2 * WL, 6 * C), BF16),
             V((2 * WL, 4 * C), F32),
             V((48, 6 * C), F32),
@@ -714,10 +689,9 @@
             V((4, 32, 128), F32),
             V((32, 128), F32),
             V((8, 32, 128), F32),
-            dma((18,)), dma((2,)), dma((2,)), dma((9,)), dma((9,)), dma((16,)), dma((16,)),
-            dma((4,)), dma((4,)), dma((4, 4)), dma((4, 4)), dma((4,)), dma((4,)),
-            dma((2, 8)), dma((2, 8)),
-            dma((2, 8)), dma((2, 8)), pltpu.SemaphoreType.REGULAR((5,)),
+            dma((9,)), dma((2,)), dma((2,)), dma((9,)), dma((9,)), dma((1,)), dma((1,)),
+            dma((4,)), dma((4,)), dma((4,)), dma((4,)), dma((1,)), dma((1,)),
+            dma((2,)), dma((2,)), dma((2,)), dma((2,)), pltpu.SemaphoreType.REGULAR((5,)),
         ],
         compiler_params=pltpu.CompilerParams(
             collective_id=0, has_side_effects=True, vmem_limit_bytes=60 * 1024 * 1024
@@ -726,7 +700,7 @@
         latents, conv_weight, conv_bias.reshape(1, C), out_weight, row_table, patch_weight,
         pos_embed, proj_weight, text_embed.reshape(1, EMB),
     )
-    return reward, gconv, gout
+    return reward.reshape(1), gconv, gout
 
 
 def solution(mesh):

time: 55.2 us -> 53.9 us (0.976)
  Pallas kernels: 49.7 us -> 48.5 us
    pallas_call x1, Pallas kernels: 49.7 us -> 48.5 us  [per_device(): pl.pallas_call(kernel, out_shape=(jax.ShapeDtypeStruct((1, 1), F32), jax....]
where the time goes in v5:
time: 53.9 us; the launch traced here: 53.7 us
  Pallas kernels  48.5 us (90%)
  local copies, waits for them, and re-layouts  2.79 us (5%)
  between operations  2.46 us (5%)
    pallas_call x1, Pallas kernels, per_device(): pl.pallas_call(kernel, out_shape=(jax.ShapeDtypeStruct((1, 1), F32), jax....  48.5 us
    unnamed x2, local copies, waits for them, and re-layouts  2.79 us

profile of v5, /device:TPU:1, one launch (start us, length us, event | category | flops | bytes accessed | tf_op | source)
XLA Modules:
  0.0 53.7 jit_solution(15951654544246574491)
XLA Ops:
  0.6 48.5 %shard_map.112 = (f32[1,1]{1,0:T(1,128)}, f32[36,256]{1,0:T(8,128)}, f32[3,2304]{1,0:T(4,128)}) custom-call(bf16[1,2,128,256]{3,2,1,0:T(8,128)(2,1)} %lat_hbm.1, bf16[2304,256]{1,0:T(8,128)(2,1)} %cw_hbm.1, f32[1,256]{1,0:T(1,128)} %bitcast.4, bf16[3,2304]{1,0:T(4,128)(2,1)} %ow_hbm.1, s32[1,224]{1,0:T(1,128)} %table_hbm.1, bf16[588,1280]{1,0:T(8,128)(2,1)} %pw_hbm.1, ...), custom_call_target="tpu_custom_call" | custom-call | tf_op jit(solution)/shard_map/pallas_call | solution.py:642
  49.8 1.4 %copy.16 = f32[36,256]{1,0:T(8,128)} copy(f32[36,256]{1,0:T(8,128)} %get-tuple-element.13) | data formatting | bytes 73728
  51.2 1.4 %copy.17 = f32[3,2304]{1,0:T(4,128)} copy(f32[3,2304]{1,0:T(4,128)} %get-tuple-element.14) | data formatting | bytes 55296

commit v6 on v5

--- a/solution.py
+++ b/solution.py
@@ -58,7 +58,7 @@
     reward_ref, gconv_ref, gout_ref,
     bias_ref, ow_ref, table_ref, text_ref,
     lat4, wl, taps, hbuf, gate, wd32, wo32, pw, pwp, pos, proj,
-    dec, dall, ct, gt, ybuf, psend, precv, igs, latt,
+    dec, dall, ct, ct2, gt, ybuf, psend, precv, igs, latt,
     g32, gbf, gcr, xbf, x32, xr, zbf, z32, zr, yb, yr,
     go2, gocr, goz, gozr, gox, goxr, goy, goyr,
     loc_sem, halo_ss, halo_rs, gat_ss, gat_rs, pool_ss, pool_rs,
@@ -311,7 +311,7 @@
     hi = jnp.maximum(nxt, lo + 1.0)
     inv = 1.0 / (hi - lo)
     lane = iota((128, 144), 1)
-    row = (4 * base + (lane >> 2)).astype(F32)
+    row = (4 * jnp.where(rk < 64, 4 * p, base) + (lane >> 2)).astype(F32)
     inside = valid & ((lane & 3) == colour) & (row >= lo) & (row < hi)
     pick = jnp.where(inside, 1.0, 0.0).astype(BF16)
     lane = iota((128, 128), 1)
@@ -338,31 +338,26 @@
 
     more = p < GROUPS - 1
     for v in range(4):
-        gather_wait(
-            v, (low_half & (q == 0) & (p > 0)) | ((q >= 2) & (q != v)),
-            jnp.where(low_half, 4 * p - 4 + v, 4 * p + v),
-        )
-        if v == 0:
-            cond = (low_half & (q != v)) | ((q >= 2) & more)
-        else:
-            cond = (low_half & (q != v)) | ((q == 3) & more)
-        gather_wait(v + 4, cond, jnp.where(low_half, 4 * p + v, 4 * p + 4 + v))
-    gather_wait(
-        8, (low_half & more) | ((q == 3) & (p < GROUPS - 2)),
-        jnp.where(low_half, 4 * p + 4, 4 * p + 8),
-    )
-
+        gather_wait(v, (q >= 2) & (q != v), 4 * p + v)
+        gather_wait(v + 4, low_half & (q != v), 4 * p + v)
+    gather_wait(4, (q >= 2) & more, 4 * p + 4)
+    gather_wait(8, low_half & more, 4 * p + 4)
+    lane16 = iota((16, 128), 1) < 64
+
+    def patch_parts(crop, turned):
+        turned[...] = jnp.concatenate([crop, jnp.zeros((64, 256), F32)], axis=0).T
+        columns = []
+        for c14 in range(14):
+            pc, pj = patch_column(c14)
+            columns.append(turned[pl.ds(pc * WL + pj, 16, stride=8), :])
+        return [
+            jnp.where(lane16, columns[2 * n], pltpu.roll(columns[2 * n + 1], 64, 1))
+            for n in range(7)
+        ]
+
+    own_rows = dall[pl.ds(jnp.where(low_half, 4, 0), 5)].reshape(80, 256)
+    own_parts = patch_parts(dot_nn(pick[0:64, 0:80], own_rows) * inv[0:64], ct)
     flood_wait(1)
-    crop = dot_nn(pick, dall[...].reshape(144, 256)) * inv
-    ct[...] = crop.T
-    lane16 = iota((16, 128), 1) < 64
-    pairs = []
-    for n in range(7):
-        pair = []
-        for c14 in (2 * n, 2 * n + 1):
-            pc, pj = patch_column(c14)
-            pair.append(ct[pl.ds(pc * WL + pj, 16, stride=8), :])
-        pairs.append(pair)
     pos_load.wait()
 
     def embed(parts, rows):
@@ -375,9 +370,7 @@
         ybuf[rows, :] = normed
         return normed, sigma
 
-    normed, sigma0 = embed(
-        [jnp.where(lane16, one_, pltpu.roll(two, 64, 1)) for one_, two in pairs], slice(0, 16)
-    )
+    normed, sigma0 = embed(own_parts, slice(0, 16))
     gsum = jnp.sum(normed, axis=0, keepdims=True)
     psend[...] = gsum
     precv[p] = gsum
@@ -387,9 +380,13 @@
             None, psend, precv.at[p], pool_ss.at[0], pool_rs.at[0], f, 4 * ((p + d) % GROUPS) + q
         )
 
-    sigma1 = embed(
-        [jnp.where(lane16, pltpu.roll(one_, 64, 1), two) for one_, two in pairs], slice(16, 32)
-    )[1]
+    for v in range(4):
+        gather_wait(v, (q == 0) & (p > 0), 4 * p - 4 + v)
+        if v > 0:
+            gather_wait(v + 4, (q == 3) & more, 4 * p + 4 + v)
+    gather_wait(8, (q == 3) & (p < GROUPS - 2), 4 * p + 8)
+    next_crop = dot_nn(pick[64:128], dall[...].reshape(144, 256)) * inv[64:128]
+    sigma1 = embed(patch_parts(next_crop, ct2), slice(16, 32))[1]
     sigma = jnp.concatenate([sigma0, sigma1], axis=0)
 
     for n in range(4):
@@ -665,6 +662,7 @@
             V((9, 16, 256), BF16),
             V((256, 128), F32),
             V((256, 128), F32),
+            V((256, 128), F32),
             V((32, CW), F32),
             V((1, CW), F32),
             V((GROUPS, 1, CW), F32),
@@ -694,12 +692,14 @@
             dma((2,)), dma((2,)), dma((2,)), dma((2,)), pltpu.SemaphoreType.REGULAR((5,)),
         ],
         compiler_params=pltpu.CompilerParams(
-            collective_id=0, has_side_effects=True, vmem_limit_bytes=60 * 1024 * 1024
+            collective_id=0, has_side_effects=True, vmem_limit_bytes=48 * 1024 * 1024
         ),
-    )(
-        latents, conv_weight, conv_bias.reshape(1, C), out_weight, row_table, patch_weight,
-        pos_embed, proj_weight, text_embed.reshape(1, EMB),
-    )
+    )(*[
+        pltpu.with_memory_space_constraint(v, pltpu.HBM) for v in (
+            latents, conv_weight, conv_bias.reshape(1, C), out_weight, row_table, patch_weight,
+            pos_embed, proj_weight, text_embed.reshape(1, EMB),
+        )
+    ])
     return reward.reshape(1), gconv, gout
 
 

time: 53.9 us -> 51.6 us (0.957)
  local copies, waits for them, and re-layouts: 2.79 us -> 1.24 us
    unnamed x2, local copies, waits for them, and re-layouts: 2.79 us -> 1.24 us
where the time goes in v6:
time: 51.6 us; the launch traced here: 51.5 us
  Pallas kernels  48 us (93%)
  between operations  2.33 us (5%)
  local copies, waits for them, and re-layouts  1.24 us (2%)
    pallas_call x1, Pallas kernels, per_device(): pl.pallas_call(kernel, out_shape=(jax.ShapeDtypeStruct((1, 1), F32), jax....  48 us
    unnamed x2, local copies, waits for them, and re-layouts  1.24 us

profile of v6, /device:TPU:1, one launch (start us, length us, event | category | flops | bytes accessed | tf_op | source)
XLA Modules:
  0.0 51.5 jit_solution(7875847663217722070)
XLA Ops:
  0.6 48.0 %shard_map.112 = (f32[1,1]{1,0:T(1,128)}, f32[36,256]{1,0:T(8,128)S(1)}, f32[3,2304]{1,0:T(4,128)S(1)}) custom-call(bf16[1,2,128,256]{3,2,1,0:T(8,128)(2,1)} %lat_hbm.1, bf16[2304,256]{1,0:T(8,128)(2,1)} %cw_hbm.1, f32[1,256]{1,0:T(1,128)} %bitcast.4, bf16[3,2304]{1,0:T(4,128)(2,1)} %ow_hbm.1, s32[1,224]{1,0:T(1,128)} %table_hbm.1, ...), custom_call_target="tpu_custom_call" | custom-call | tf_op jit(solution)/shard_map/pallas_call | solution.py:639
  49.2 0.6 %copy.16 = f32[36,256]{1,0:T(8,128)} copy(f32[36,256]{1,0:T(8,128)S(1)} %get-tuple-element.13) | data formatting | bytes 73728
  49.8 0.6 %copy.17 = f32[3,2304]{1,0:T(4,128)} copy(f32[3,2304]{1,0:T(4,128)S(1)} %get-tuple-element.14) | data formatting | bytes 55296

commit v7 on v6

--- a/solution.py
+++ b/solution.py
@@ -57,7 +57,7 @@
     lat_hbm, cw_hbm, bias_hbm, ow_hbm, table_hbm, pw_hbm, pos_hbm, proj_hbm, text_hbm,
     reward_ref, gconv_ref, gout_ref,
     bias_ref, ow_ref, table_ref, text_ref,
-    lat4, wl, taps, hbuf, gate, wd32, wo32, pw, pwp, pos, proj,
+    lat4, wl, taps, hbuf, gate, wd32, wo32, pw, pwp, pwpt, pos, proj, projt,
     dec, dall, ct, ct2, gt, ybuf, psend, precv, igs, latt,
     g32, gbf, gcr, xbf, x32, xr, zbf, z32, zr, yb, yr,
     go2, gocr, goz, gozr, gox, goxr, goy, goyr,
@@ -357,7 +357,6 @@
 
     own_rows = dall[pl.ds(jnp.where(low_half, 4, 0), 5)].reshape(80, 256)
     own_parts = patch_parts(dot_nn(pick[0:64, 0:80], own_rows) * inv[0:64], ct)
-    flood_wait(1)
     pos_load.wait()
 
     def embed(parts, rows):
@@ -375,6 +374,7 @@
     psend[...] = gsum
     precv[p] = gsum
 
+    flood_wait(1)
     for d in range(1, GROUPS):
         send_part(
             None, psend, precv.at[p], pool_ss.at[0], pool_rs.at[0], f, 4 * ((p + d) % GROUPS) + q
@@ -396,6 +396,13 @@
         gate[:, cut] = sig * (1.0 + total * (1.0 - sig))
     for n in range(4):
         latt[:, n * WL:(n + 1) * WL] = lat4[n].astype(F32).T.astype(BF16)
+    proj_load.wait()
+    for n in range(CW // 256):
+        cut = slice(n * 256, (n + 1) * 256)
+        projt[:, cut] = proj[cut, :].astype(F32).T.astype(BF16)
+    for n in range(KP // 128):
+        cut = slice(n * 128, (n + 1) * 128)
+        pwpt[:, cut] = pwp[cut, :].astype(F32).T.astype(BF16)
     text_load.wait()
     text = text_ref[...]
     text2 = jnp.sum(text * text, axis=1, keepdims=True) + 1e-06
@@ -407,7 +414,6 @@
         pooled = pooled + precv[n]
     pooled = pooled * (1.0 / 256.0)
 
-    proj_load.wait()
 
     def two_rows(v):
         top = iota((16, v.shape[1]), 0)
@@ -424,7 +430,7 @@
     reward = numer * scale
     reward_ref[...] = reward
     dproj = -LOSS_SCALE * (text * scale - projected * (reward / norm2))
-    dunit = jnp.sum(dot_nt(two_rows(dproj), proj[...]), axis=0, keepdims=True)
+    dunit = jnp.sum(dot_nn(two_rows(dproj), projt[...]), axis=0, keepdims=True)
 
     def norm_back(dy, y, sg):
         m1 = jnp.mean(dy, axis=1, keepdims=True)
@@ -433,7 +439,7 @@
 
     dpooled = norm_back(dunit, unit, psigma) * (1.0 / 256.0)
     demb = norm_back(dpooled, ybuf[...], sigma)
-    dpat = dot_nt(jnp.concatenate(split2(demb), axis=0), pwp[...])
+    dpat = dot_nn(jnp.concatenate(split2(demb), axis=0), pwpt[...])
     dpat = dpat[0:32] + dpat[32:64]
     for n in range(7):
         d0 = dpat[0:16, n * 128:(n + 1) * 128]
@@ -482,10 +488,9 @@
 
     def put_grad(a, b, value):
         at = (3 * a + b) * C
-        for half in range(2):
-            part = value[:, half * 128:(half + 1) * 128]
-            g32[half, at:at + C, :] = part
-            gbf[half, at:at + C, :] = part.astype(BF16)
+        left, right = value[:, 0:128], value[:, 128:256]
+        g32[at:at + C, :] = jnp.where(core == 0, left, right)
+        gbf[at:at + C, :] = jnp.where(core == 0, right, left).astype(BF16)
 
     outer = [
         jnp.concatenate([cols_of[0][b], cols_of[1][b] + cols_of[2][b], cols_of[3][b]], axis=0)
@@ -503,12 +508,15 @@
         send_part(None, goz, gozr.at[z], z_ss.at[0], z_rs.at[0], f, x * 16 + zd * 2 + y_lo)
 
     main = []
+    outer = jnp.concatenate(outer, axis=1)
+    inner = jnp.concatenate(inner, axis=1)
     for a, start, stop, terms in ((0, 0, 3, outer), (1, 1, 3, inner), (2, 1, 4, outer)):
+        value = dot_nn(latt[:, start * WL:stop * WL], terms)
         for b in range(3):
-            put_grad(a, b, dot_nn(latt[:, start * WL:stop * WL], terms[b]))
+            put_grad(a, b, value[:, b * C:(b + 1) * C])
         rows = pl.ds(a * 768, 768)
         main.append(
-            send(None, gbf.at[1 - core, rows], gcr.at[rows], c_ss.at[a], c_rs.at[a], fc, s)
+            send(None, gbf.at[rows], gcr.at[rows], c_ss.at[a], c_rs.at[a], fc, s)
         )
 
     mine = jnp.where(core == 0, x, y)
@@ -518,8 +526,8 @@
         sd = jnp.where(core == 0, n * 16 + z * 2 + y_lo, x * 16 + z * 2 + n % 2)
         return fd, sd
 
-    def halves_sum(half, start, count):
-        return g32[half, start:start + count, :] + gcr[start:start + count, :].astype(F32)
+    def halves_sum(start, count):
+        return g32[start:start + count, :] + gcr[start:start + count, :].astype(F32)
 
     for w in range(4):
         for part in range(2):
@@ -533,7 +541,7 @@
             def along_x():
                 for n in (2 * part, 2 * part + 1):
                     total = jnp.concatenate(
-                        [halves_sum(0, n * 576 + zd * 72, 72) for zd in (w, w + 4)], axis=0
+                        [halves_sum(n * 576 + zd * 72, 72) for zd in (w, w + 4)], axis=0
                     )
                     x32[n, w] = total
                     xbf[n, w] = total.astype(BF16)
@@ -541,7 +549,7 @@
             @pl.when(core == 1)
             def along_y():
                 units = [
-                    halves_sum(1, (2 * part + h) * 576 + zd * 72, 72)
+                    halves_sum((2 * part + h) * 576 + zd * 72, 72)
                     for zd in (w, w + 4) for h in range(2)
                 ]
                 for n in range(2):
@@ -656,8 +664,10 @@
             V((48, C), F32),
             V((588, CW), BF16),
             V((KP, CW), BF16),
+            V((CW, KP), BF16),
             V((32, CW), BF16),
             V((CW, EMB), BF16),
+            V((EMB, CW), BF16),
             V((16, 256), BF16),
             V((9, 16, 256), BF16),
             V((256, 128), F32),
@@ -668,8 +678,8 @@
             V((GROUPS, 1, CW), F32),
             V((3, 32, 256), F32),
             V((C, 4 * WL), BF16),
-            V((2, 9 * C, 128), F32),
-            V((2, 9 * C, 128), BF16),
+            V((9 * C, 128), F32),
+            V((9 * C, 128), BF16),
             V((9 * C, 128), BF16),
             V((4, 4, 144, 128), BF16),
             V((4, 4, 144, 128), F32),

time: 51.6 us -> 50.9 us (0.986)
  Pallas kernels: 48 us -> 47.3 us
    pallas_call x1, Pallas kernels: 48 us -> 47.3 us  [per_device(): pl.pallas_call(kernel, out_shape=(jax.ShapeDtypeStruct((1, 1), F32), jax....]
where the time goes in v7:
time: 50.9 us; the launch traced here: 50.8 us
  Pallas kernels  47.3 us (93%)
  between operations  2.33 us (5%)
  local copies, waits for them, and re-layouts  1.24 us (2%)
    pallas_call x1, Pallas kernels, per_device(): pl.pallas_call(kernel, out_shape=(jax.ShapeDtypeStruct((1, 1), F32), jax....  47.3 us
    unnamed x2, local copies, waits for them, and re-layouts  1.24 us

profile of v7, /device:TPU:1, one launch (start us, length us, event | category | flops | bytes accessed | tf_op | source)
XLA Modules:
  0.0 50.8 jit_solution(8872386177307502731)
XLA Ops:
  0.6 47.3 %shard_map.112 = (f32[1,1]{1,0:T(1,128)}, f32[36,256]{1,0:T(8,128)S(1)}, f32[3,2304]{1,0:T(4,128)S(1)}) custom-call(bf16[1,2,128,256]{3,2,1,0:T(8,128)(2,1)} %lat_hbm.1, bf16[2304,256]{1,0:T(8,128)(2,1)} %cw_hbm.1, f32[1,256]{1,0:T(1,128)} %bitcast.4, bf16[3,2304]{1,0:T(4,128)(2,1)} %ow_hbm.1, s32[1,224]{1,0:T(1,128)} %table_hbm.1, ...), custom_call_target="tpu_custom_call" | custom-call | tf_op jit(solution)/shard_map/pallas_call | solution.py:647
  48.5 0.6 %copy.16 = f32[36,256]{1,0:T(8,128)} copy(f32[36,256]{1,0:T(8,128)S(1)} %get-tuple-element.13) | data formatting | bytes 73728
  49.1 0.6 %copy.17 = f32[3,2304]{1,0:T(4,128)} copy(f32[3,2304]{1,0:T(4,128)S(1)} %get-tuple-element.14) | data formatting | bytes 55296

commit v8 on v7

--- a/solution.py
+++ b/solution.py
@@ -287,14 +287,14 @@
     def gather_send(n, cond, target, slot):
         send(cond, dec, dall.at[slot], gat_ss.at[n], gat_rs.at[slot], f, target)
 
+    gather_send(5, (q == 0) & (p > 0), 4 * p - 4, 8)
+    gather_send(6, (q == 0) & (p > 0), 4 * p - 3, 8)
+    gather_send(7, (q == 0) & (p > 0), 4 * p - 2, 4)
     for d in range(1, 4):
         qd = (q + d) % 4
         gather_send(d - 1, None, 4 * p + qd, jnp.where(qd < 2, q + 4, q))
     gather_send(3, p < GROUPS - 1, 4 * p + 4, q)
     gather_send(4, p > 0, 4 * p - 1, q + 4)
-    gather_send(5, (q == 0) & (p > 0), 4 * p - 4, 8)
-    gather_send(6, (q == 0) & (p > 0), 4 * p - 3, 8)
-    gather_send(7, (q == 0) & (p > 0), 4 * p - 2, 4)
     gather_send(8, (q == 0) & (p > 1), 4 * p - 5, 8)
 
     rk = iota((128, 1), 0)
@@ -375,10 +375,11 @@
     precv[p] = gsum
 
     flood_wait(1)
-    for d in range(1, GROUPS):
-        send_part(
-            None, psend, precv.at[p], pool_ss.at[0], pool_rs.at[0], f, 4 * ((p + d) % GROUPS) + q
-        )
+    steps = [(dx, dz) for dx in range(4) for dz in range(4) if dx or dz]
+    steps.sort(key=lambda d: -min(d[0], 4 - d[0]) - 2 * min(d[1], 4 - d[1]))
+    for dx, dz in steps:
+        other = ((x + dx) % 4) * 4 + (z // 2 + dz) % 4
+        send_part(None, psend, precv.at[p], pool_ss.at[0], pool_rs.at[0], f, 4 * other + q)
 
     for v in range(4):
         gather_wait(v, (q == 0) & (p > 0), 4 * p - 4 + v)

time: 50.9 us -> 50.9 us (level)
  no operation moved by 1% of the time
where the time goes in v8:
time: 50.9 us; the launch traced here: 50.8 us
  Pallas kernels  47.3 us (93%)
  between operations  2.33 us (5%)
  local copies, waits for them, and re-layouts  1.24 us (2%)
    pallas_call x1, Pallas kernels, per_device(): pl.pallas_call(kernel, out_shape=(jax.ShapeDtypeStruct((1, 1), F32), jax....  47.3 us
    unnamed x2, local copies, waits for them, and re-layouts  1.24 us

profile of v8, /device:TPU:1, one launch (start us, length us, event | category | flops | bytes accessed | tf_op | source)
XLA Modules:
  0.0 50.8 jit_solution(1980839046055178202)
XLA Ops:
  0.6 47.3 %shard_map.112 = (f32[1,1]{1,0:T(1,128)}, f32[36,256]{1,0:T(8,128)S(1)}, f32[3,2304]{1,0:T(4,128)S(1)}) custom-call(bf16[1,2,128,256]{3,2,1,0:T(8,128)(2,1)} %lat_hbm.1, bf16[2304,256]{1,0:T(8,128)(2,1)} %cw_hbm.1, f32[1,256]{1,0:T(1,128)} %bitcast.4, bf16[3,2304]{1,0:T(4,128)(2,1)} %ow_hbm.1, s32[1,224]{1,0:T(1,128)} %table_hbm.1, ...), custom_call_target="tpu_custom_call" | custom-call | tf_op jit(solution)/shard_map/pallas_call | solution.py:648
  48.5 0.6 %copy.16 = f32[36,256]{1,0:T(8,128)} copy(f32[36,256]{1,0:T(8,128)S(1)} %get-tuple-element.13) | data formatting | bytes 73728
  49.1 0.6 %copy.17 = f32[3,2304]{1,0:T(4,128)} copy(f32[3,2304]{1,0:T(4,128)S(1)} %get-tuple-element.14) | data formatting | bytes 55296

commit v9 on v8

--- a/solution.py
+++ b/solution.py
@@ -106,8 +106,8 @@
     def yc_device(idx):
         return (idx // 4) * 2 + idx % 2, x * 16 + z * 2 + (idx // 2) % 2
 
-    for d in range(1, 8):
-        greet(None, *yc_device((yc + d) % 8))
+    greet(None, y_hi * 2 + 1 - core, s)
+    greet(None, (1 - y_hi) * 2 + core, s)
     y = y_hi * 2 + y_lo
 
     def one(cond):
@@ -117,7 +117,7 @@
         one(s > 0) + one(s < N_SLAB - 1)
         + 3 + one(p < GROUPS - 1) + one(p > 0)
         + one((q == 0) & (p > 0)) * 3
-        + 3 + 2 + 7
+        + 3 + 2 + 2
     )
 
     loads = []

time: 50.9 us -> 50.5 us (level)
  no operation moved by 1% of the time
where the time goes in v9:
time: 50.5 us; the launch traced here: 50.4 us
  Pallas kernels  46.8 us (93%)
  between operations  2.33 us (5%)
  local copies, waits for them, and re-layouts  1.24 us (2%)
    pallas_call x1, Pallas kernels, per_device(): pl.pallas_call(kernel, out_shape=(jax.ShapeDtypeStruct((1, 1), F32), jax....  46.8 us
    unnamed x2, local copies, waits for them, and re-layouts  1.24 us

profile of v9, /device:TPU:1, one launch (start us, length us, event | category | flops | bytes accessed | tf_op | source)
XLA Modules:
  0.0 50.4 jit_solution(3922594616738972645)
XLA Ops:
  0.6 46.8 %shard_map.112 = (f32[1,1]{1,0:T(1,128)}, f32[36,256]{1,0:T(8,128)S(1)}, f32[3,2304]{1,0:T(4,128)S(1)}) custom-call(bf16[1,2,128,256]{3,2,1,0:T(8,128)(2,1)} %lat_hbm.1, bf16[2304,256]{1,0:T(8,128)(2,1)} %cw_hbm.1, f32[1,256]{1,0:T(1,128)} %bitcast.4, bf16[3,2304]{1,0:T(4,128)(2,1)} %ow_hbm.1, s32[1,224]{1,0:T(1,128)} %table_hbm.1, ...), custom_call_target="tpu_custom_call" | custom-call | tf_op jit(solution)/shard_map/pallas_call | solution.py:648
  48.0 0.6 %copy.16 = f32[36,256]{1,0:T(8,128)} copy(f32[36,256]{1,0:T(8,128)S(1)} %get-tuple-element.13) | data formatting | bytes 73728
  48.6 0.6 %copy.17 = f32[3,2304]{1,0:T(4,128)} copy(f32[3,2304]{1,0:T(4,128)S(1)} %get-tuple-element.14) | data formatting | bytes 55296
